TPU v7x, 128 devices: a whole 4x4x4 slice. The times are simulated.
128 devices in a mesh: dp: 16 (over y, z), expert: 8 (over x, core).
Axes of the slice: x: 4, y: 4, z: 4, core: 2. Of those that a mesh axis runs over, the one named last changes fastest.
Arguments:
- grad_out: bfloat16 [16384, 6144], P(('dp', 'expert')), may hold values from -6 to 6
- routes: int32 [16384, 2], P(('dp', 'expert')), may hold values from 0 to 31, all different within a row; in each aligned block of 128 rows (0 to 127, 128 to 255, ...) at most 9 rows name the same one
- loss_weight: int32 [16384], P(('dp', 'expert')), may hold values from 1 to 4
- saved_input: bfloat16 [32, 1152, 6144], P('dp', None, 'expert'), may hold values from -6 to 6
- saved_gate: bfloat16 [32, 1152, 1024], P('dp', None, 'expert'), may hold values from -8 to 8
- saved_up: bfloat16 [32, 1152, 1024], P('dp', None, 'expert'), may hold values from -6 to 6
- w_gate: bfloat16 [32, 6144, 1024], P('dp', 'expert'), may hold values from -0.1875 to 0.1875
- w_up: bfloat16 [32, 6144, 1024], P('dp', 'expert'), may hold values from -0.1875 to 0.1875
- w_down: bfloat16 [32, 1024, 6144], P('dp', None, 'expert'), may hold values from -0.078125 to 0.078125
Outputs:
- grad_input: bfloat16 [16384, 6144], P(('dp', 'expert'))
- grad_gate: bfloat16 [32, 6144, 1024], P('dp', 'expert')
- grad_up: bfloat16 [32, 6144, 1024], P('dp', 'expert')
- grad_down: bfloat16 [32, 1024, 6144], P('dp', None, 'expert')
Inputs may be any that keep to these rules, and one draw needn't show every extreme that they name: `routes`: each row names two different experts; among the rows of one device no expert is named more than 9 times, and some device names some expert exactly 9 times.
All inputs are finite; a program needn't handle non-finite values.
Results may differ from a plain program's by a relative error of at most 0.0061.
Values may be sent and summed in bfloat16 or wider, within the bound.
No kernel may reach another device: no remote copies, remote signals or barrier semaphores. Data moves between devices by JAX's collectives and lax.ppermute only.
A program may use at most 192 MiB of HBM per device.

v0:
```python
import jax
import jax.numpy as jnp
from jax import lax
from jax.experimental import pallas as pl
from jax.experimental.pallas import tpu as pltpu
from jax.sharding import PartitionSpec as P

X_CHIPS = 4
VMEM = 48 * 2**20
CORES = 2
BF16 = jnp.bfloat16
F32 = jnp.float32


def pairs(dx, dc):
    return [
        (x * CORES + c, ((x + dx) % X_CHIPS) * CORES + (c + dc) % CORES)
        for x in range(X_CHIPS)
        for c in range(CORES)
    ]


def along_x(v, dx):
    return lax.ppermute(v, "expert", pairs(dx, 0))


def swap_core(v):
    return lax.ppermute(v, "expert", pairs(0, 1))


def dot(a, b, ca, cb):
    return lax.dot_general(a, b, (((ca,), (cb,)), ((), ())), preferred_element_type=F32)


def call(kernel, scalars, grid, in_specs, out_specs, out_shape, operands, scratch=(), cost=1000):
    return pl.pallas_call(
        kernel,
        grid_spec=pltpu.PrefetchScalarGridSpec(
            num_scalar_prefetch=1,
            grid=grid,
            in_specs=in_specs,
            out_specs=out_specs,
            scratch_shapes=scratch,
        ),
        out_shape=out_shape,
        compiler_params=pltpu.CompilerParams(vmem_limit_bytes=VMEM),
        cost_estimate=pl.CostEstimate(flops=1000, bytes_accessed=cost, transcendentals=0),
    )(scalars, *operands)


def out(shape, dtype):
    return jax.ShapeDtypeStruct(shape, dtype)


def unused(refs):
    return [pl.BlockSpec(memory_space=pl.ANY)] * len(refs)


def both_saved(where, gate, up, after):
    rows, lanes = gate.shape
    tile = rows // 2

    def kernel(where_ref, g_ref, u_ref, *refs):
        refs[-1][0] = g_ref[...]
        refs[-1][1] = u_ref[...]

    spec = pl.BlockSpec((tile, lanes), lambda i, s: (i, 0))
    return call(
        kernel,
        where,
        (2,),
        [spec, spec] + unused(after),
        pl.BlockSpec((2, tile, lanes), lambda i, s: (0, i, 0)),
        out((2, rows, lanes), gate.dtype),
        (gate, up, *after),
    )


def forwarded(where, ahead, behind, after):
    _, rows, lanes = ahead.shape
    tile = rows // 2

    def kernel(where_ref, a_ref, b_ref, *refs):
        refs[-2][...] = a_ref[...]
        refs[-1][...] = b_ref[...]

    made = pl.BlockSpec((tile, lanes), lambda i, s: (i, 0))
    return call(
        kernel,
        where,
        (2,),
        [
            pl.BlockSpec((None, tile, lanes), lambda i, s: (0, i, 0)),
            pl.BlockSpec((None, tile, lanes), lambda i, s: (1, i, 0)),
        ]
        + unused(after),
        [made, made],
        [out((rows, lanes), ahead.dtype)] * 2,
        (ahead, behind, *after),
    )


def hidden_partials(where, e, dispatched, w_down, after):
    slots, cols = dispatched.shape
    units = w_down.shape[1]
    rows = slots // X_CHIPS
    block = rows // CORES
    tile = 256

    def kernel(where_ref, a_ref, w_ref, *refs):
        keep_ref, give_ref, acc_ref = refs[-3:]
        x, c = where_ref[0], where_ref[1]
        acc_ref[...] = dot(a_ref[...], w_ref[...], 1, 1)
        for i in range(X_CHIPS):
            base = (x + i) % X_CHIPS * rows
            keep_ref[i] = acc_ref[pl.ds(pl.multiple_of(base + c * block, block), block), :]
            give = acc_ref[pl.ds(pl.multiple_of(base + (1 - c) * block, block), block), :]
            give_ref[i] = give.astype(BF16)

    return call(
        kernel,
        where,
        (units // tile,),
        [
            pl.BlockSpec((slots, cols), lambda i, s: (0, 0)),
            pl.BlockSpec((None, tile, cols), lambda i, s: (e, i, 0)),
        ]
        + unused(after),
        [pl.BlockSpec((X_CHIPS, block, tile), lambda i, s: (0, 0, i))] * 2,
        [out((X_CHIPS, block, units), F32), out((X_CHIPS, block, units), BF16)],
        (dispatched, w_down, *after),
        [pltpu.VMEM((slots, tile), F32)],
    )


def pair_sums(where, keep, received, after):
    chips, block, units = keep.shape
    tile = 48

    def kernel(where_ref, k_ref, r_ref, *refs):
        outs = refs[-chips:]
        for i in range(chips):
            outs[i][...] = (k_ref[i] + r_ref[i].astype(F32)).astype(outs[i].dtype)

    return call(
        kernel,
        where,
        (block // tile,),
        [pl.BlockSpec((chips, tile, units), lambda i, s: (0, i, 0))] * 2 + unused(after),
        [pl.BlockSpec((tile, units), lambda i, s: (i, 0))] * chips,
        [out((block, units), F32 if i == 0 else BF16) for i in range(chips)],
        (keep, received, *after),
    )


def chip_sums(where, own, received, after):
    block, units = own.shape
    tile = 48
    count = len(received)

    def kernel(where_ref, o_ref, *refs):
        total = o_ref[...]
        for r in refs[:count]:
            total = total + r[...].astype(F32)
        refs[-1][...] = total.astype(BF16)

    spec = pl.BlockSpec((tile, units), lambda i, s: (i, 0))
    return call(
        kernel,
        where,
        (block // tile,),
        [spec] * (1 + count) + unused(after),
        spec,
        out((block, units), BF16),
        (own, *received, *after),
    )


def slot_gradient(where, e, pieces, saved, w_gate, w_up, after):
    count = len(pieces)
    block, units_all = pieces[0].shape
    flat = [r for v in saved for r in v]
    lanes = flat[0].shape[-1]
    slots = block * count
    cols = w_gate.shape[1]
    pair = CORES * block
    tile = 256
    chunk = 48

    def kernel(where_ref, *refs):
        piece_refs = refs[:count]
        saved_refs = refs[count : 3 * count]
        wg_ref, wu_ref = refs[3 * count : 3 * count + 2]
        dg_ref, du_ref, h_ref, sg_ref, dgs_ref, dus_ref, part_ref = refs[-7:]
        k = pl.program_id(0)
        x, c = where_ref[0], where_ref[1]

        for i in range(X_CHIPS):

            @pl.when(k == i)
            def _(i=i):
                for near, core in ((True, c), (False, 1 - c)):
                    rows_here = pl.ds(pl.multiple_of(core * block, block), block)
                    part_ref[rows_here, :] = piece_refs[i if near else X_CHIPS + i][...]

        @pl.when(k < X_CHIPS)
        def _():
            base = (x - k + X_CHIPS) % X_CHIPS * pair

            @pl.loop(0, pair // chunk)
            def _(r):
                here = pl.ds(pl.multiple_of(r * chunk, chunk), chunk)
                whole = pl.ds(pl.multiple_of(base + r * chunk, chunk), chunk)
                for j in range(count):
                    unit = (x - j % X_CHIPS + X_CHIPS) % X_CHIPS * CORES + (c if j < X_CHIPS else 1 - c)
                    span = pl.ds(pl.multiple_of(unit * lanes, lanes), lanes)
                    g = saved_refs[2 * j][here, :].astype(F32)
                    u = saved_refs[2 * j + 1][here, :].astype(F32)
                    part = part_ref[here, span].astype(F32)
                    sig = 0.5 * jnp.tanh(0.5 * g) + 0.5
                    act = g * sig
                    h_ref[here, span] = (act * u).astype(BF16)
                    dg = (part * (u * sig * (1.0 + g * (1.0 - sig)))).astype(BF16)
                    du = (part * act).astype(BF16)
                    dg_ref[here, span] = dg
                    du_ref[here, span] = du
                    dgs_ref[whole, span] = dg
                    dus_ref[whole, span] = du

        @pl.when(k >= X_CHIPS)
        def _():
            total = dot(dgs_ref[...], wg_ref[...], 1, 1) + dot(dus_ref[...], wu_ref[...], 1, 1)
            sg_ref[...] = total.astype(BF16)

    def rows(k, s):
        return (s[0] - jnp.minimum(k, X_CHIPS - 1) + X_CHIPS) % X_CHIPS

    def column(k):
        return jnp.maximum(k - X_CHIPS, 0)

    specs, operands = [], []
    for arrays in saved:
        for which, v in enumerate(arrays):
            if v.ndim == 3:
                specs.append(
                    pl.BlockSpec(
                        (None, pair, lanes),
                        lambda k, s, which=which: (which, e * X_CHIPS + rows(k, s), 0),
                    )
                )
            else:
                specs.append(pl.BlockSpec((pair, lanes), lambda k, s: (e * X_CHIPS + rows(k, s), 0)))
            operands.append(v)
    weight = pl.BlockSpec((None, tile, units_all), lambda k, s: (e, column(k), 0))
    return call(
        kernel,
        where,
        (X_CHIPS + cols // tile,),
        [pl.BlockSpec((block, units_all), lambda k, s: (0, 0))] * count + specs + [weight] * 2 + unused(after),
        [pl.BlockSpec((pair, units_all), lambda k, s: (rows(k, s), 0))] * 3
        + [pl.BlockSpec((slots, tile), lambda k, s: (0, column(k)))],
        [out((slots, units_all), BF16)] * 3 + [out((slots, cols), BF16)],
        (*pieces, *operands, w_gate, w_up, *after),
        [pltpu.VMEM((slots, units_all), BF16)] * 2 + [pltpu.VMEM((pair, units_all), BF16)],
        50_000_000,
    )


def down_gradient(where, h0, h1, d0, d1):
    slots, cols = d0.shape
    units = h0.shape[1]
    tile = 256

    def kernel(where_ref, h0_ref, h1_ref, d0_ref, d1_ref, o_ref):
        for e, (h_ref, d_ref) in enumerate(((h0_ref, d0_ref), (h1_ref, d1_ref))):

            @pl.when(pl.program_id(0) == e)
            def _(h_ref=h_ref, d_ref=d_ref):
                o_ref[...] = dot(h_ref[...], d_ref[...], 0, 0).astype(BF16)

    whole = pl.BlockSpec((slots, cols), lambda e, k, s: (0, 0))
    last = units // tile - 1
    return call(
        kernel,
        where,
        (2, units // tile),
        [
            pl.BlockSpec((slots, tile), lambda e, k, s: (0, jnp.where(e == 0, k, last))),
            pl.BlockSpec((slots, tile), lambda e, k, s: (0, jnp.where(e == 0, 0, k))),
            whole,
            whole,
        ],
        pl.BlockSpec((None, tile, cols), lambda e, k, s: (e, k, 0)),
        out((2, units, cols), BF16),
        (h0, h1, d0, d1),
    )


def up_gradients(where, saved_input, dg0, du0, dg1, du1, after):
    experts, slots, cols = saved_input.shape
    units = dg0.shape[1]
    tile = 256

    def kernel(where_ref, x_ref, dg0_ref, du0_ref, dg1_ref, du1_ref, *refs):
        og_ref, ou_ref = refs[-2:]
        for e, (g_ref, u_ref) in enumerate(((dg0_ref, du0_ref), (dg1_ref, du1_ref))):
            @pl.when(pl.program_id(0) == e)
            def _(g_ref=g_ref, u_ref=u_ref):
                og_ref[...] = dot(x_ref[...], g_ref[...], 0, 0).astype(BF16)
                ou_ref[...] = dot(x_ref[...], u_ref[...], 0, 0).astype(BF16)

    whole = pl.BlockSpec((slots, units), lambda e, k, s: (0, 0))
    made = pl.BlockSpec((None, tile, units), lambda e, k, s: (e, k, 0))
    return call(
        kernel,
        where,
        (experts, cols // tile),
        [pl.BlockSpec((None, slots, tile), lambda e, k, s: (e, 0, k))] + [whole] * 4 + unused(after),
        [made, made],
        [out((experts, cols, units), BF16)] * 2,
        (saved_input, dg0, du0, dg1, du1, *after),
    )


def body(grad_out, routes, loss_weight, saved_input, saved_gate, saved_up, w_gate, w_up, w_down):
    groups = lax.axis_size("dp")
    splits = lax.axis_size("expert")
    pos = lax.axis_index("expert")
    my_x, my_c = pos // CORES, pos % CORES
    where = jnp.stack([my_x, my_c]).astype(jnp.int32)
    experts = w_gate.shape[0]
    tokens = grad_out.shape[0]
    width = grad_out.shape[1]
    cols = width // splits
    slots = saved_input.shape[1]
    cap = slots // (groups * splits)
    lanes = saved_gate.shape[2]

    chosen = routes.reshape(-1)
    order = jnp.arange(chosen.shape[0], dtype=jnp.int32)
    same = (chosen[:, None] == chosen[None, :]) & (order[:, None] < order[None, :])
    rank = jnp.sum(same.astype(jnp.int32), axis=0)
    row = (chosen % experts) * slots + (chosen // experts) * (splits * cap) + pos * cap + rank
    row = row.reshape(tokens, 2).T
    code = jnp.concatenate([row // 64, row % 64], axis=0).astype(BF16)
    code = jnp.pad(code, ((0, 4), (0, cols - tokens)))
    code = jnp.concatenate([code, code], axis=1)

    scaled = (grad_out.astype(F32) * loss_weight.astype(F32)[:, None] * 0.25).astype(BF16)
    near, far = [], []
    for dx in range(X_CHIPS):
        piece = lax.dynamic_slice(
            scaled, (0, (my_x + dx) % X_CHIPS * (CORES * cols)), (tokens, CORES * cols)
        )
        piece = jnp.concatenate([piece, code], axis=0)
        if dx:
            piece = along_x(piece, dx)
        near.append(lax.dynamic_slice(piece, (0, my_c * cols), (tokens + 8, cols)))
        far.append(swap_core(lax.dynamic_slice(piece, (0, (1 - my_c) * cols), (tokens + 8, cols))))
    gathered = jnp.stack(near + far)
    codes = gathered[:, tokens : tokens + 4, :tokens].astype(jnp.int32)
    row_of = (codes[:, :2] * 64 + codes[:, 2:]).transpose(1, 0, 2).reshape(2, splits * tokens)
    gathered = gathered[:, :tokens].reshape(splits * tokens, cols)

    index = jnp.arange(slots, dtype=jnp.int32)[:, None]
    placed = [
        ((row_of[0][None, :] == index + e * slots) | (row_of[1][None, :] == index + e * slots)).astype(BF16)
        for e in range(experts)
    ]
    outgoing = [dot(placed[e], gathered, 1, 0).astype(BF16) for e in range(experts)]
    dispatched = [
        lax.all_to_all(
            o.reshape(groups, splits * cap, cols), "dp", split_axis=0, concat_axis=0, tiled=True
        ).reshape(slots, cols)
        for o in outgoing
    ]

    both = both_saved(
        where,
        saved_gate.reshape(experts * slots, lanes),
        saved_up.reshape(experts * slots, lanes),
        (gathered,),
    )
    ahead, behind = along_x(both, 1), along_x(both, 3)
    pick_a, pick_b = forwarded(where, ahead, behind, ())
    across = (along_x(pick_a, 1), along_x(pick_b, 3))
    held = [(both, both), (ahead, ahead), across, (behind, behind)]
    both_o, ahead_o, behind_o = swap_core(both), swap_core(ahead), swap_core(behind)
    across_o = (swap_core(across[0]), swap_core(across[1]))
    held += [(both_o, both_o), (ahead_o, ahead_o), across_o, (behind_o, behind_o)]

    def partials(e, after, after_pair):
        keep, give = hidden_partials(where, e, dispatched[e], w_down, after)
        return pair_sums(where, keep, swap_core(give), after_pair)

    def exchanged(sent):
        return [along_x(v, dx) for dx, v in enumerate(sent, 1)]

    def spread(own):
        pieces = [own] + [along_x(own, dx) for dx in range(1, X_CHIPS)]
        return pieces + [swap_core(v) for v in pieces]

    def give_back(slot_grad):
        returned = lax.all_to_all(
            slot_grad.reshape(groups, splits * cap, cols), "dp", split_axis=0, concat_axis=0, tiled=True
        )
        return returned.reshape(slots, cols)

    first0, *sent0 = partials(0, (both_o, ahead_o, behind_o, *across), ())
    own0 = chip_sums(where, first0, exchanged(sent0), across_o)
    pieces0 = spread(own0)
    first1, *sent1 = partials(1, (own0,), ())
    own1 = chip_sums(where, first1, exchanged(sent1), ())
    dgate0, dup0, hidden0, slot_grad0 = slot_gradient(where, 0, pieces0, held, w_gate, w_up, (own1,))
    returned0 = give_back(slot_grad0)
    pieces1 = spread(own1)
    dgate1, dup1, hidden1, slot_grad1 = slot_gradient(where, 1, pieces1, held, w_gate, w_up, ())
    returned1 = give_back(slot_grad1)
    back0 = dot(placed[0], returned0, 0, 0)
    grad_down = down_gradient(where, hidden0, hidden1, *dispatched)
    grad_gate, grad_up = up_gradients(where, saved_input, dgate0, dup0, dgate1, dup1, (back0,))
    returned1, grad_down, grad_gate, grad_up = lax.optimization_barrier(
        (returned1, grad_down, grad_gate, grad_up)
    )
    back = [back0, dot(placed[1], returned1, 0, 0)]

    combined = sum(back).astype(BF16).reshape(CORES, X_CHIPS, tokens, cols)
    mine, other = combined[0], swap_core(combined[1])
    grad_input = jnp.zeros((tokens, width), BF16)
    for dx in range(X_CHIPS):
        for core, v in ((my_c, mine), (1 - my_c, other)):
            piece = along_x(v[dx], X_CHIPS - dx) if dx else v[dx]
            at = ((my_x + dx) % X_CHIPS * CORES + core) * cols
            grad_input = lax.dynamic_update_slice(grad_input, piece, (0, at))
    return (grad_input, grad_gate, grad_up, grad_down)


def solution(mesh):
    return jax.shard_map(
        body,
        mesh=mesh,
        in_specs=(
            P(("dp", "expert"), None),
            P(("dp", "expert"), None),
            P(("dp", "expert")),
            P("dp", None, "expert"),
            P("dp", None, "expert"),
            P("dp", None, "expert"),
            P("dp", "expert", None),
            P("dp", "expert", None),
            P("dp", None, "expert"),
        ),
        out_specs=(
            P(("dp", "expert"), None),
            P("dp", "expert", None),
            P("dp", "expert", None),
            P("dp", None, "expert"),
        ),
        check_vma=False,
    )
```

profile of v0, /device:TPU:1, one launch (start us, length us, event | category | flops | bytes accessed | tf_op | source)
XLA Modules:
  0.0 289.0 jit_solution(8884829619252098917)
XLA Ops:
  3.7 1.9 multiply_convert_fusion
  5.9 2.1 collective-permute-start
  8.0 2.5 collective-permute-start.1
  13.3 4.9 %collective-permute-done = bf16[136,1536]{1,0:T(8,128)(2,1)S(1)} collective-permute-done((bf16[136,1536]{1,0:T(8,128)(2,1)S(1)}, bf16[136,1536]{1,0:T(8,128)(2,1)S(1)}, u32[]{:S(2)}, u32[]{:S(2)}) %collective-permute-start) | collective-permute-done | bytes 417824 | tf_op jit(solution)/shard_map/ppermute | solution.py:24
  18.2 1.8 collective-permute-start.4
  20.0 8.5 %collective-permute-done.1 = bf16[136,1536]{1,0:T(8,128)(2,1)S(1)} collective-permute-done((bf16[136,1536]{1,0:T(8,128)(2,1)S(1)}, bf16[136,1536]{1,0:T(8,128)(2,1)S(1)}, u32[]{:S(2)}, u32[]{:S(2)}) %collective-permute-start.1) | collective-permute-done | bytes 417824 | tf_op jit(solution)/shard_map/ppermute | solution.py:24
  36.5 3.7 %fusion.8 = bf16[1152,768]{1,0:T(8,128)(2,1)} fusion(bf16[1024,768]{1,0:T(8,128)(2,1)S(1)} %bitcast.52, s32[1024]{0:T(1024)S(1)} %bitcast.65, s32[1024]{0:T(1024)S(1)} %bitcast.61), kind=kOutput, calls=%fused_computation.9 | convolution fusion | flops 1816363008 | bytes 3350528 | tf_op jit(solution)/shard_map/dot_general | solution.py:32
  40.2 7.9 %all-to-all-start = ((bf16[16,72,768]{2,1,0:T(8,128)(2,1)}), bf16[16,72,768]{2,1,0:T(8,128)(2,1)}, u32[]{:S(2)}, u32[]{:S(2)}) async-start(bf16[16,72,768]{2,1,0:T(8,128)(2,1)} %bitcast.15), calls=%async_computation | async-start | bytes 3538944 | tf_op jit(solution)/shard_map/all_to_all | solution.py:372
  49.2 13.5 %collective-permute-done.10.b_ref.refs_14_.refs_15_ = bf16[2,2304,128]{2,1,0:T(8,128)(2,1)} collective-permute-done((bf16[2,2304,128]{2,1,0:T(8,128)(2,1)}, bf16[2,2304,128]{2,1,0:T(8,128)(2,1)}, u32[]{:S(2)}, u32[]{:S(2)}) %collective-permute-start.10) | collective-permute-done | bytes 1179680 | tf_op jit(solution)/shard_map/ppermute | solution.py:24
  66.4 2.7 shard_map.121
  69.0 2.7 collective-permute-start.13
  71.7 3.4 %fusion.7 = bf16[1152,768]{1,0:T(8,128)(2,1)} fusion(bf16[1024,768]{1,0:T(8,128)(2,1)S(1)} %bitcast.53, s32[1024]{0:T(1024)S(1)} %bitcast.66, s32[1024]{0:T(1024)S(1)} %bitcast.62, s32[1152]{0:T(1024)S(1)} %iota_add_fusion), kind=kOutput, calls=%fused_computation.8 | convolution fusion | flops 1816363008 | bytes 3355136 | tf_op jit(solution)/shard_map/dot_general | solution.py:32
  75.1 8.2 %all-to-all-start.1 = ((bf16[16,72,768]{2,1,0:T(8,128)(2,1)}), bf16[16,72,768]{2,1,0:T(8,128)(2,1)}, u32[]{:S(2)}, u32[]{:S(2)}) async-start(bf16[16,72,768]{2,1,0:T(8,128)(2,1)} %bitcast.57), calls=%async_computation.1 | async-start | bytes 3538944 | tf_op jit(solution)/shard_map/all_to_all | solution.py:372
  83.4 2.1 collective-permute-done.12.refs_3_.refs_12_
  85.5 6.7 %shard_map.122 = (f32[4,144,1024]{2,1,0:T(8,128)}, bf16[4,144,1024]{2,1,0:T(8,128)(2,1)S(1)}) custom-call(s32[2]{0:T(128)S(1)} %pad_add_fusion.where_ref, bf16[1152,768]{1,0:T(8,128)(2,1)} %bitcast.16.a_ref.d0_ref, bf16[2,1024,768]{2,1,0:T(8,128)(2,1)} %w_ref.3, bf16[2,2304,128]{2,1,0:T(8,128)(2,1)S(1)} %collective-permute-done.7.refs_0_.refs_16_.refs_17_, ...), custom_call_target="tpu_custom_call" | custom-call | flops 1000 | bytes 1000 | tf_op jit(solution)/shard_map/pallas_call | solution.py:36
  93.6 2.7 collective-permute-done.14.r_ref
  96.3 1.7 copy-done.7
  99.1 3.8 %collective-permute-start.16 = (bf16[144,1024]{1,0:T(8,128)(2,1)S(1)}, bf16[144,1024]{1,0:T(8,128)(2,1)S(1)}, u32[]{:S(2)}, u32[]{:S(2)}) collective-permute-start(bf16[144,1024]{1,0:T(8,128)(2,1)S(1)} %get-tuple-element.38), channel_id=1, source_target_pairs={{0,4},{1,5},{2,6},{3,7},{4,0},{5,1},{6,2},{7,3},{8,12},{9,13},{10,... | collective-permute-start | bytes 884744 | tf_op jit(solution)/shard_map/ppermute | solution.py:24
  103.0 5.7 %collective-permute-done.15.refs_0_ = bf16[144,1024]{1,0:T(8,128)(2,1)S(1)} collective-permute-done((bf16[144,1024]{1,0:T(8,128)(2,1)S(1)}, bf16[144,1024]{1,0:T(8,128)(2,1)S(1)}, u32[]{:S(2)}, u32[]{:S(2)}) %collective-permute-start.15) | collective-permute-done | bytes 294944 | tf_op jit(solution)/shard_map/ppermute | solution.py:24
  108.7 7.4 %collective-permute-done.16.refs_1_ = bf16[144,1024]{1,0:T(8,128)(2,1)S(1)} collective-permute-done((bf16[144,1024]{1,0:T(8,128)(2,1)S(1)}, bf16[144,1024]{1,0:T(8,128)(2,1)S(1)}, u32[]{:S(2)}, u32[]{:S(2)}) %collective-permute-start.16) | collective-permute-done | bytes 294944 | tf_op jit(solution)/shard_map/ppermute | solution.py:24
  116.8 5.6 %shard_map.125 = (f32[4,144,1024]{2,1,0:T(8,128)S(1)}, bf16[4,144,1024]{2,1,0:T(8,128)(2,1)S(1)}) custom-call(s32[2]{0:T(128)S(1)} %pad_add_fusion.where_ref, bf16[1152,768]{1,0:T(8,128)(2,1)} %bitcast.20.a_ref.d1_ref, bf16[2,1024,768]{2,1,0:T(8,128)(2,1)} %w_ref.3, bf16[144,1024]{1,0:T(8,128)(2,1)S(1)} %shard_map.124.refs_0_), custom_call_target="tpu_custom_call" | custom-call | flops 1000 | bytes 1000 | tf_op jit(solution)/shard_map/pallas_call | solution.py:36
  123.7 3.1 %collective-permute-start.21 = (bf16[144,1024]{1,0:T(8,128)(2,1)S(1)}, bf16[144,1024]{1,0:T(8,128)(2,1)S(1)}, u32[]{:S(2)}, u32[]{:S(2)}) collective-permute-start(bf16[144,1024]{1,0:T(8,128)(2,1)S(1)} %shard_map.124.refs_0_), channel_id=1, source_target_pairs={{0,4},{1,5},{2,6},{3,7},{4,0},{5,1},{6,2},{7,3},{8,12},{9,13},{10,... | collective-permute-start | bytes 884744 | tf_op jit(solution)/shard_map/ppermute | solution.py:24
  130.4 3.1 %collective-permute-done.20.refs_1_ = bf16[144,1024]{1,0:T(8,128)(2,1)S(1)} collective-permute-done((bf16[144,1024]{1,0:T(8,128)(2,1)S(1)}, bf16[144,1024]{1,0:T(8,128)(2,1)S(1)}, u32[]{:S(2)}, u32[]{:S(2)}) %collective-permute-start.20) | collective-permute-done | bytes 294944 | tf_op jit(solution)/shard_map/ppermute | solution.py:24
  133.5 1.8 collective-permute-start.23
  135.3 5.0 %collective-permute-done.21.refs_2_ = bf16[144,1024]{1,0:T(8,128)(2,1)S(1)} collective-permute-done((bf16[144,1024]{1,0:T(8,128)(2,1)S(1)}, bf16[144,1024]{1,0:T(8,128)(2,1)S(1)}, u32[]{:S(2)}, u32[]{:S(2)}) %collective-permute-start.21) | collective-permute-done | bytes 294944 | tf_op jit(solution)/shard_map/ppermute | solution.py:24
  140.3 1.8 collective-permute-start.24
  142.1 4.1 %collective-permute-done.28.refs_0_ = bf16[144,1024]{1,0:T(8,128)(2,1)S(1)} collective-permute-done((bf16[144,1024]{1,0:T(8,128)(2,1)S(1)}, bf16[144,1024]{1,0:T(8,128)(2,1)S(1)}, u32[]{:S(2)}, u32[]{:S(2)}) %collective-permute-start.28) | collective-permute-done | bytes 294944 | tf_op jit(solution)/shard_map/ppermute | solution.py:24
  147.0 5.9 %collective-permute-done.29.refs_1_ = bf16[144,1024]{1,0:T(8,128)(2,1)S(1)} collective-permute-done((bf16[144,1024]{1,0:T(8,128)(2,1)S(1)}, bf16[144,1024]{1,0:T(8,128)(2,1)S(1)}, u32[]{:S(2)}, u32[]{:S(2)}) %collective-permute-start.29) | collective-permute-done | bytes 294944 | tf_op jit(solution)/shard_map/ppermute | solution.py:24
  155.0 15.1 %shard_map.128 = (bf16[1152,1024]{1,0:T(8,128)(2,1)}, bf16[1152,1024]{1,0:T(8,128)(2,1)}, bf16[1152,1024]{1,0:T(8,128)(2,1)}, bf16[1152,768]{1,0:T(8,128)(2,1)}) custom-call(s32[2]{0:T(128)S(1)} %pad_add_fusion.where_ref, bf16[144,1024]{1,0:T(8,128)(2,1)S(1)} %shard_map.124.refs_0_, bf16[144,1024]{1,0:T(8,128)(2,1)S(1)} %collective-permute-done.20.refs_1_, ...), custom_call_target="tpu_custom_call" | custom-call | flops 1000 | bytes 50000000 | tf_op jit(solution)/shard_map/pallas_call | solution.py:36
  170.1 7.9 %all-to-all-start.2 = ((bf16[16,72,768]{2,1,0:T(8,128)(2,1)}), bf16[16,72,768]{2,1,0:T(8,128)(2,1)S(1)}, u32[]{:S(2)}, u32[]{:S(2)}) async-start(bf16[16,72,768]{2,1,0:T(8,128)(2,1)} %bitcast.58), calls=%async_computation.2 | async-start | bytes 3538944 | tf_op jit(solution)/shard_map/all_to_all | solution.py:404
  178.1 2.9 collective-permute-start.32
  182.3 4.9 %collective-permute-done.31.refs_1_ = bf16[144,1024]{1,0:T(8,128)(2,1)S(1)} collective-permute-done((bf16[144,1024]{1,0:T(8,128)(2,1)S(1)}, bf16[144,1024]{1,0:T(8,128)(2,1)S(1)}, u32[]{:S(2)}, u32[]{:S(2)}) %collective-permute-start.31) | collective-permute-done | bytes 294944 | tf_op jit(solution)/shard_map/ppermute | solution.py:24
  187.2 2.6 collective-permute-start.35
  189.7 3.8 %collective-permute-done.32.refs_2_ = bf16[144,1024]{1,0:T(8,128)(2,1)S(1)} collective-permute-done((bf16[144,1024]{1,0:T(8,128)(2,1)S(1)}, bf16[144,1024]{1,0:T(8,128)(2,1)S(1)}, u32[]{:S(2)}, u32[]{:S(2)}) %collective-permute-start.32) | collective-permute-done | bytes 294944 | tf_op jit(solution)/shard_map/ppermute | solution.py:24
  193.6 1.7 collective-permute-start.36
  195.2 9.8 %collective-permute-start.37 = (bf16[144,1024]{1,0:T(8,128)(2,1)S(1)}, bf16[144,1024]{1,0:T(8,128)(2,1)S(1)}, u32[]{:S(2)}, u32[]{:S(2)}) collective-permute-start(bf16[144,1024]{1,0:T(8,128)(2,1)S(1)} %collective-permute-done.33.refs_3_), channel_id=1, source_target_pairs={{0,1},{1,0},{2,3},{3,2},{4,5},{5,4},{6,7},{7,6},{8,9},{9,8},{10,11... | collective-permute-start | bytes 884744 | tf_op jit(solution)/shard_map/ppermute | solution.py:28
  206.3 15.3 %shard_map.129 = (bf16[1152,1024]{1,0:T(8,128)(2,1)}, bf16[1152,1024]{1,0:T(8,128)(2,1)}, bf16[1152,1024]{1,0:T(8,128)(2,1)}, bf16[1152,768]{1,0:T(8,128)(2,1)}) custom-call(s32[2]{0:T(128)S(1)} %pad_add_fusion.where_ref, bf16[144,1024]{1,0:T(8,128)(2,1)S(1)} %shard_map.127.refs_26_.refs_0_, bf16[144,1024]{1,0:T(8,128)(2,1)S(1)} %collective-permute-done.31.refs_1_, ...), custom_call_target="tpu_custom_call" | custom-call | flops 1000 | bytes 50000000 | tf_op jit(solution)/shard_map/pallas_call | solution.py:36
  222.8 6.8 %all-to-all-start.3 = ((bf16[16,72,768]{2,1,0:T(8,128)(2,1)}), bf16[16,72,768]{2,1,0:T(8,128)(2,1)}, u32[]{:S(2)}, u32[]{:S(2)}) async-start(bf16[16,72,768]{2,1,0:T(8,128)(2,1)} %bitcast.59), calls=%async_computation.3 | async-start | bytes 3538944 | tf_op jit(solution)/shard_map/all_to_all | solution.py:404
  229.6 10.7 %shard_map.130 = bf16[2,1024,768]{2,1,0:T(8,128)(2,1)} custom-call(s32[2]{0:T(128)S(1)} %pad_add_fusion.where_ref, bf16[1152,1024]{1,0:T(8,128)(2,1)S(1)} %copy-done.8, bf16[1152,1024]{1,0:T(8,128)(2,1)} %get-tuple-element.49.h1_ref, bf16[1152,768]{1,0:T(8,128)(2,1)} %bitcast.16.a_ref.d0_ref, bf16[1152,768]{1,0:T(8,128)(2,1)} %bitcast.20.a_ref.d1_ref), custom_call_target="tpu_custom_call" | custom-call | flops 1000 | bytes 1000 | tf_op jit(solution)/shard_map/pallas_call | solution.py:36
  240.4 4.1 %fusion.3.refs_0_ = f32[1024,768]{1,0:T(8,128)} fusion(bf16[1152,768]{1,0:T(8,128)(2,1)S(1)} %bitcast.56, s32[1024]{0:T(1024)S(1)} %bitcast.67, s32[1024]{0:T(1024)S(1)} %bitcast.63), kind=kOutput, calls=%fused_computation.6 | convolution fusion | flops 1815478272 | bytes 4923392 | tf_op jit(solution)/shard_map/dot_general | solution.py:32
  244.5 13.9 %shard_map.131 = (bf16[2,768,1024]{2,1,0:T(8,128)(2,1)}, bf16[2,768,1024]{2,1,0:T(8,128)(2,1)}) custom-call(s32[2]{0:T(128)S(1)} %pad_add_fusion.where_ref, bf16[2,1152,768]{2,1,0:T(8,128)(2,1)} %x_ref.1, bf16[1152,1024]{1,0:T(8,128)(2,1)S(1)} %copy-done.5, bf16[1152,1024]{1,0:T(8,128)(2,1)S(1)} %copy-done.6, bf16[1152,1024]{1,0:T(8,128)(2,1)} %get-tuple-element.52.dg1_ref, ...), custom_call_target="tpu_custom_call" | custom-call | flops 1000 | bytes 1000 | tf_op jit(solution)/shard_map/pallas_call | solution.py:36
  258.4 4.2 %add_convert_fusion = bf16[1024,768]{1,0:T(8,128)(2,1)S(1)} fusion(f32[1024,768]{1,0:T(8,128)S(1)} %copy-done.11, bf16[1152,768]{1,0:T(8,128)(2,1)} %bitcast.24, s32[1024]{0:T(1024)S(1)} %bitcast.68, s32[1024]{0:T(1024)S(1)} %bitcast.64, s32[1152]{0:T(1024)S(1)} %iota_add_fusion), kind=kOutput, calls=%fused_computation.10 | convolution fusion | flops 1817051136 | bytes 6500864 | tf_op jit(solution)/shard_map/dot_general | solution.py:32
  265.2 2.2 collective-permute-start.39
  268.1 2.1 collective-permute-start.40
  270.2 1.8 collective-permute-start.42
  272.1 7.7 %collective-permute-done.40 = bf16[128,768]{1,0:T(8,128)(2,1)S(1)} collective-permute-done((bf16[128,768]{1,0:T(8,128)(2,1)S(1)}, bf16[128,768]{1,0:T(8,128)(2,1)S(1)}, u32[]{:S(2)}, u32[]{:S(2)}) %collective-permute-start.40) | collective-permute-done | bytes 196640 | tf_op jit(solution)/shard_map/ppermute | solution.py:24
  279.8 3.1 %collective-permute-done.42 = bf16[128,768]{1,0:T(8,128)(2,1)S(1)} collective-permute-done((bf16[128,768]{1,0:T(8,128)(2,1)S(1)}, bf16[128,768]{1,0:T(8,128)(2,1)S(1)}, u32[]{:S(2)}, u32[]{:S(2)}) %collective-permute-start.42) | collective-permute-done | bytes 196640 | tf_op jit(solution)/shard_map/ppermute | solution.py:24
  283.0 4.7 %collective-permute-done.44 = bf16[128,768]{1,0:T(8,128)(2,1)S(1)} collective-permute-done((bf16[128,768]{1,0:T(8,128)(2,1)S(1)}, bf16[128,768]{1,0:T(8,128)(2,1)S(1)}, u32[]{:S(2)}, u32[]{:S(2)}) %collective-permute-start.44) | collective-permute-done | bytes 196640 | tf_op jit(solution)/shard_map/ppermute | solution.py:24
  (152 shorter events, 38.4 us)
Async XLA Ops:
  5.9 12.3 %collective-permute-start = (bf16[136,1536]{1,0:T(8,128)(2,1)S(1)}, bf16[136,1536]{1,0:T(8,128)(2,1)S(1)}, u32[]{:S(2)}, u32[]{:S(2)}) collective-permute-start(bf16[136,1536]{1,0:T(8,128)(2,1)S(1)} %get-tuple-element.74), channel_id=1, source_target_pairs={{0,2},{1,3},{2,4},{3,5},{4,6},{5,7},{6,0},{7,1},{8,10},{9,11},{10,... | collective-permute-start | bytes 1253384 | tf_op jit(solution)/shard_map/ppermute | solution.py:24
  8.0 20.4 %collective-permute-start.1 = (bf16[136,1536]{1,0:T(8,128)(2,1)S(1)}, bf16[136,1536]{1,0:T(8,128)(2,1)S(1)}, u32[]{:S(2)}, u32[]{:S(2)}) collective-permute-start(bf16[136,1536]{1,0:T(8,128)(2,1)S(1)} %get-tuple-element.75), channel_id=1, source_target_pairs={{0,4},{1,5},{2,6},{3,7},{4,0},{5,1},{6,2},{7,3},{8,12},{9,13},{10,... | collective-permute-start | bytes 1253384 | tf_op jit(solution)/shard_map/ppermute | solution.py:24
  10.4 19.6 %collective-permute-start.2 = (bf16[136,1536]{1,0:T(8,128)(2,1)S(1)}, bf16[136,1536]{1,0:T(8,128)(2,1)S(1)}, u32[]{:S(2)}, u32[]{:S(2)}) collective-permute-start(bf16[136,1536]{1,0:T(8,128)(2,1)S(1)} %get-tuple-element.73), channel_id=1, source_target_pairs={{0,6},{1,7},{2,0},{3,1},{4,2},{5,3},{6,4},{7,5},{8,14},{9,15},{10,... | collective-permute-start | bytes 1253384 | tf_op jit(solution)/shard_map/ppermute | solution.py:24
  11.6 18.7 %collective-permute-start.3 = (bf16[136,768]{1,0:T(8,128)(2,1)S(1)}, bf16[136,768]{1,0:T(8,128)(2,1)S(1)}, u32[]{:S(2)}, u32[]{:S(2)}) collective-permute-start(bf16[136,768]{1,0:T(8,128)(2,1)S(1)} %constant_dynamic-slice_fusion.3), channel_id=1, source_target_pairs={{0,1},{1,0},{2,3},{3,2},{4,5},{5,4},{6,7},{7,6},{8,9},{9,8},{10,11... | collective-permute-start | bytes 626696 | tf_op jit(solution)/shard_map/ppermute | solution.py:28
  18.2 12.1 %collective-permute-start.4 = (bf16[136,768]{1,0:T(8,128)(2,1)S(1)}, bf16[136,768]{1,0:T(8,128)(2,1)S(1)}, u32[]{:S(2)}, u32[]{:S(2)}) collective-permute-start(bf16[136,768]{1,0:T(8,128)(2,1)S(1)} %constant_dynamic-slice_fusion.2), channel_id=1, source_target_pairs={{0,1},{1,0},{2,3},{3,2},{4,5},{5,4},{6,7},{7,6},{8,9},{9,8},{10,11... | collective-permute-start | bytes 626696 | tf_op jit(solution)/shard_map/ppermute | solution.py:28
  28.5 2.7 collective-permute-start.5
  35.0 27.7 %collective-permute-start.10 = (bf16[2,2304,128]{2,1,0:T(8,128)(2,1)}, bf16[2,2304,128]{2,1,0:T(8,128)(2,1)}, u32[]{:S(2)}, u32[]{:S(2)}) collective-permute-start(bf16[2,2304,128]{2,1,0:T(8,128)(2,1)} %shard_map.120.refs_8_.refs_9_), channel_id=1, source_target_pairs={{0,6},{1,7},{2,0},{3,1},{4,2},{5,3},{6,4},{7,5},{8,14},{9,15},{10,... | collective-permute-start | bytes 3538952 | tf_op jit(solution)/shard_map/ppermute | solution.py:24
  36.4 28.4 %collective-permute-start.8 = (bf16[2,2304,128]{2,1,0:T(8,128)(2,1)}, bf16[2,2304,128]{2,1,0:T(8,128)(2,1)}, u32[]{:S(2)}, u32[]{:S(2)}) collective-permute-start(bf16[2,2304,128]{2,1,0:T(8,128)(2,1)} %shard_map.120.refs_8_.refs_9_), channel_id=1, source_target_pairs={{0,2},{1,3},{2,4},{3,5},{4,6},{5,7},{6,0},{7,1},{8,10},{9,11},{10,... | collective-permute-start | bytes 3538952 | tf_op jit(solution)/shard_map/ppermute | solution.py:24
  40.2 34.9 %all-to-all-start = ((bf16[16,72,768]{2,1,0:T(8,128)(2,1)}), bf16[16,72,768]{2,1,0:T(8,128)(2,1)}, u32[]{:S(2)}, u32[]{:S(2)}) async-start(bf16[16,72,768]{2,1,0:T(8,128)(2,1)} %bitcast.15), calls=%async_computation | async-start | bytes 3538944 | tf_op jit(solution)/shard_map/all_to_all | solution.py:372
  48.1 35.2 %collective-permute-start.7 = (bf16[2,2304,128]{2,1,0:T(8,128)(2,1)}, bf16[2,2304,128]{2,1,0:T(8,128)(2,1)S(1)}, u32[]{:S(2)}, u32[]{:S(2)}) collective-permute-start(bf16[2,2304,128]{2,1,0:T(8,128)(2,1)} %shard_map.120.refs_8_.refs_9_), channel_id=1, source_target_pairs={{0,1},{1,0},{2,3},{3,2},{4,5},{5,4},{6,7},{7,6},{8,9},{9,8},{10,11... | collective-permute-start | bytes 3538952 | tf_op jit(solution)/shard_map/ppermute | solution.py:28
  62.7 22.8 %collective-permute-start.11 = (bf16[2,2304,128]{2,1,0:T(8,128)(2,1)}, bf16[2,2304,128]{2,1,0:T(8,128)(2,1)S(1)}, u32[]{:S(2)}, u32[]{:S(2)}) collective-permute-start(bf16[2,2304,128]{2,1,0:T(8,128)(2,1)} %collective-permute-done.10.b_ref.refs_14_.refs_15_), channel_id=1, source_target_pairs={{0,1},{1,0},{2,3},{3,2},{4,5},{5,4},{6,7},{7,6},{8,9},{9,8},{10,11... | collective-permute-start | bytes 3538952 | tf_op jit(solution)/shard_map/ppermute | solution.py:28
  64.8 20.7 %collective-permute-start.9 = (bf16[2,2304,128]{2,1,0:T(8,128)(2,1)}, bf16[2,2304,128]{2,1,0:T(8,128)(2,1)S(1)}, u32[]{:S(2)}, u32[]{:S(2)}) collective-permute-start(bf16[2,2304,128]{2,1,0:T(8,128)(2,1)} %collective-permute-done.8.a_ref.refs_10_.refs_11_), channel_id=1, source_target_pairs={{0,1},{1,0},{2,3},{3,2},{4,5},{5,4},{6,7},{7,6},{8,9},{9,8},{10,11... | collective-permute-start | bytes 3538952 | tf_op jit(solution)/shard_map/ppermute | solution.py:28
  69.0 16.5 %collective-permute-start.12 = (bf16[2304,128]{1,0:T(8,128)(2,1)}, bf16[2304,128]{1,0:T(8,128)(2,1)}, u32[]{:S(2)}, u32[]{:S(2)}) collective-permute-start(bf16[2304,128]{1,0:T(8,128)(2,1)} %get-tuple-element.32), channel_id=1, source_target_pairs={{0,2},{1,3},{2,4},{3,5},{4,6},{5,7},{6,0},{7,1},{8,10},{9,11},{10,... | collective-permute-start | bytes 1769480 | tf_op jit(solution)/shard_map/ppermute | solution.py:24
  69.0 16.5 %collective-permute-start.13 = (bf16[2304,128]{1,0:T(8,128)(2,1)}, bf16[2304,128]{1,0:T(8,128)(2,1)}, u32[]{:S(2)}, u32[]{:S(2)}) collective-permute-start(bf16[2304,128]{1,0:T(8,128)(2,1)} %get-tuple-element.33), channel_id=1, source_target_pairs={{0,6},{1,7},{2,0},{3,1},{4,2},{5,3},{6,4},{7,5},{8,14},{9,15},{10,... | collective-permute-start | bytes 1769480 | tf_op jit(solution)/shard_map/ppermute | solution.py:24
  75.1 41.6 %all-to-all-start.1 = ((bf16[16,72,768]{2,1,0:T(8,128)(2,1)}), bf16[16,72,768]{2,1,0:T(8,128)(2,1)}, u32[]{:S(2)}, u32[]{:S(2)}) async-start(bf16[16,72,768]{2,1,0:T(8,128)(2,1)} %bitcast.57), calls=%async_computation.1 | async-start | bytes 3538944 | tf_op jit(solution)/shard_map/all_to_all | solution.py:372
  92.2 4.1 %collective-permute-start.14 = (bf16[4,144,1024]{2,1,0:T(8,128)(2,1)S(1)}, bf16[4,144,1024]{2,1,0:T(8,128)(2,1)S(1)}, u32[]{:S(2)}, u32[]{:S(2)}) collective-permute-start(bf16[4,144,1024]{2,1,0:T(8,128)(2,1)S(1)} %get-tuple-element.35), channel_id=1, source_target_pairs={{0,1},{1,0},{2,3},{3,2},{4,5},{5,4},{6,7},{7,6},{8,9},{9,8},{10,11... | collective-permute-start | bytes 3538952 | tf_op jit(solution)/shard_map/ppermute | solution.py:28
  93.1 9.9 %collective-permute-start.18 = (bf16[2304,128]{1,0:T(8,128)(2,1)}, bf16[2304,128]{1,0:T(8,128)(2,1)S(1)}, u32[]{:S(2)}, u32[]{:S(2)}) collective-permute-start(bf16[2304,128]{1,0:T(8,128)(2,1)} %collective-permute-done.12.refs_3_.refs_12_), channel_id=1, source_target_pairs={{0,1},{1,0},{2,3},{3,2},{4,5},{5,4},{6,7},{7,6},{8,9},{9,8},{10,11... | collective-permute-start | bytes 1769480 | tf_op jit(solution)/shard_map/ppermute | solution.py:28
  93.2 9.8 %collective-permute-start.19 = (bf16[2304,128]{1,0:T(8,128)(2,1)}, bf16[2304,128]{1,0:T(8,128)(2,1)S(1)}, u32[]{:S(2)}, u32[]{:S(2)}) collective-permute-start(bf16[2304,128]{1,0:T(8,128)(2,1)} %collective-permute-done.13.refs_4_.refs_13_), channel_id=1, source_target_pairs={{0,1},{1,0},{2,3},{3,2},{4,5},{5,4},{6,7},{7,6},{8,9},{9,8},{10,11... | collective-permute-start | bytes 1769480 | tf_op jit(solution)/shard_map/ppermute | solution.py:28
  99.0 9.6 %collective-permute-start.15 = (bf16[144,1024]{1,0:T(8,128)(2,1)S(1)}, bf16[144,1024]{1,0:T(8,128)(2,1)S(1)}, u32[]{:S(2)}, u32[]{:S(2)}) collective-permute-start(bf16[144,1024]{1,0:T(8,128)(2,1)S(1)} %get-tuple-element.37), channel_id=1, source_target_pairs={{0,2},{1,3},{2,4},{3,5},{4,6},{5,7},{6,0},{7,1},{8,10},{9,11},{10,... | collective-permute-start | bytes 884744 | tf_op jit(solution)/shard_map/ppermute | solution.py:24
  99.1 16.9 %collective-permute-start.16 = (bf16[144,1024]{1,0:T(8,128)(2,1)S(1)}, bf16[144,1024]{1,0:T(8,128)(2,1)S(1)}, u32[]{:S(2)}, u32[]{:S(2)}) collective-permute-start(bf16[144,1024]{1,0:T(8,128)(2,1)S(1)} %get-tuple-element.38), channel_id=1, source_target_pairs={{0,4},{1,5},{2,6},{3,7},{4,0},{5,1},{6,2},{7,3},{8,12},{9,13},{10,... | collective-permute-start | bytes 884744 | tf_op jit(solution)/shard_map/ppermute | solution.py:24
  103.0 13.1 %collective-permute-start.17 = (bf16[144,1024]{1,0:T(8,128)(2,1)S(1)}, bf16[144,1024]{1,0:T(8,128)(2,1)S(1)}, u32[]{:S(2)}, u32[]{:S(2)}) collective-permute-start(bf16[144,1024]{1,0:T(8,128)(2,1)S(1)} %get-tuple-element.39), channel_id=1, source_target_pairs={{0,6},{1,7},{2,0},{3,1},{4,2},{5,3},{6,4},{7,5},{8,14},{9,15},{10,... | collective-permute-start | bytes 884744 | tf_op jit(solution)/shard_map/ppermute | solution.py:24
  122.4 4.4 %collective-permute-start.27 = (bf16[4,144,1024]{2,1,0:T(8,128)(2,1)S(1)}, bf16[4,144,1024]{2,1,0:T(8,128)(2,1)S(1)}, u32[]{:S(2)}, u32[]{:S(2)}) collective-permute-start(bf16[4,144,1024]{2,1,0:T(8,128)(2,1)S(1)} %get-tuple-element.41), channel_id=1, source_target_pairs={{0,1},{1,0},{2,3},{3,2},{4,5},{5,4},{6,7},{7,6},{8,9},{9,8},{10,11... | collective-permute-start | bytes 3538952 | tf_op jit(solution)/shard_map/ppermute | solution.py:28
  123.7 9.8 %collective-permute-start.20 = (bf16[144,1024]{1,0:T(8,128)(2,1)S(1)}, bf16[144,1024]{1,0:T(8,128)(2,1)S(1)}, u32[]{:S(2)}, u32[]{:S(2)}) collective-permute-start(bf16[144,1024]{1,0:T(8,128)(2,1)S(1)} %shard_map.124.refs_0_), channel_id=1, source_target_pairs={{0,2},{1,3},{2,4},{3,5},{4,6},{5,7},{6,0},{7,1},{8,10},{9,11},{10,... | collective-permute-start | bytes 884744 | tf_op jit(solution)/shard_map/ppermute | solution.py:24
  123.7 16.5 %collective-permute-start.21 = (bf16[144,1024]{1,0:T(8,128)(2,1)S(1)}, bf16[144,1024]{1,0:T(8,128)(2,1)S(1)}, u32[]{:S(2)}, u32[]{:S(2)}) collective-permute-start(bf16[144,1024]{1,0:T(8,128)(2,1)S(1)} %shard_map.124.refs_0_), channel_id=1, source_target_pairs={{0,4},{1,5},{2,6},{3,7},{4,0},{5,1},{6,2},{7,3},{8,12},{9,13},{10,... | collective-permute-start | bytes 884744 | tf_op jit(solution)/shard_map/ppermute | solution.py:24
  126.8 13.5 %collective-permute-start.22 = (bf16[144,1024]{1,0:T(8,128)(2,1)S(1)}, bf16[144,1024]{1,0:T(8,128)(2,1)S(1)}, u32[]{:S(2)}, u32[]{:S(2)}) collective-permute-start(bf16[144,1024]{1,0:T(8,128)(2,1)S(1)} %shard_map.124.refs_0_), channel_id=1, source_target_pairs={{0,6},{1,7},{2,0},{3,1},{4,2},{5,3},{6,4},{7,5},{8,14},{9,15},{10,... | collective-permute-start | bytes 884744 | tf_op jit(solution)/shard_map/ppermute | solution.py:24
  127.9 18.3 %collective-permute-start.28 = (bf16[144,1024]{1,0:T(8,128)(2,1)S(1)}, bf16[144,1024]{1,0:T(8,128)(2,1)S(1)}, u32[]{:S(2)}, u32[]{:S(2)}) collective-permute-start(bf16[144,1024]{1,0:T(8,128)(2,1)S(1)} %get-tuple-element.43), channel_id=1, source_target_pairs={{0,2},{1,3},{2,4},{3,5},{4,6},{5,7},{6,0},{7,1},{8,10},{9,11},{10,... | collective-permute-start | bytes 884744 | tf_op jit(solution)/shard_map/ppermute | solution.py:24
  129.4 23.5 %collective-permute-start.29 = (bf16[144,1024]{1,0:T(8,128)(2,1)S(1)}, bf16[144,1024]{1,0:T(8,128)(2,1)S(1)}, u32[]{:S(2)}, u32[]{:S(2)}) collective-permute-start(bf16[144,1024]{1,0:T(8,128)(2,1)S(1)} %get-tuple-element.44), channel_id=1, source_target_pairs={{0,4},{1,5},{2,6},{3,7},{4,0},{5,1},{6,2},{7,3},{8,12},{9,13},{10,... | collective-permute-start | bytes 884744 | tf_op jit(solution)/shard_map/ppermute | solution.py:24
  133.5 21.0 %collective-permute-start.23 = (bf16[144,1024]{1,0:T(8,128)(2,1)S(1)}, bf16[144,1024]{1,0:T(8,128)(2,1)S(1)}, u32[]{:S(2)}, u32[]{:S(2)}) collective-permute-start(bf16[144,1024]{1,0:T(8,128)(2,1)S(1)} %shard_map.124.refs_0_), channel_id=1, source_target_pairs={{0,1},{1,0},{2,3},{3,2},{4,5},{5,4},{6,7},{7,6},{8,9},{9,8},{10,11... | collective-permute-start | bytes 884744 | tf_op jit(solution)/shard_map/ppermute | solution.py:28
  140.3 13.5 %collective-permute-start.30 = (bf16[144,1024]{1,0:T(8,128)(2,1)S(1)}, bf16[144,1024]{1,0:T(8,128)(2,1)S(1)}, u32[]{:S(2)}, u32[]{:S(2)}) collective-permute-start(bf16[144,1024]{1,0:T(8,128)(2,1)S(1)} %get-tuple-element.45), channel_id=1, source_target_pairs={{0,6},{1,7},{2,0},{3,1},{4,2},{5,3},{6,4},{7,5},{8,14},{9,15},{10,... | collective-permute-start | bytes 884744 | tf_op jit(solution)/shard_map/ppermute | solution.py:24
  140.3 14.3 %collective-permute-start.24 = (bf16[144,1024]{1,0:T(8,128)(2,1)S(1)}, bf16[144,1024]{1,0:T(8,128)(2,1)S(1)}, u32[]{:S(2)}, u32[]{:S(2)}) collective-permute-start(bf16[144,1024]{1,0:T(8,128)(2,1)S(1)} %collective-permute-done.20.refs_1_), channel_id=1, source_target_pairs={{0,1},{1,0},{2,3},{3,2},{4,5},{5,4},{6,7},{7,6},{8,9},{9,8},{10,11... | collective-permute-start | bytes 884744 | tf_op jit(solution)/shard_map/ppermute | solution.py:28
  146.1 8.4 %collective-permute-start.25 = (bf16[144,1024]{1,0:T(8,128)(2,1)S(1)}, bf16[144,1024]{1,0:T(8,128)(2,1)S(1)}, u32[]{:S(2)}, u32[]{:S(2)}) collective-permute-start(bf16[144,1024]{1,0:T(8,128)(2,1)S(1)} %collective-permute-done.21.refs_2_), channel_id=1, source_target_pairs={{0,1},{1,0},{2,3},{3,2},{4,5},{5,4},{6,7},{7,6},{8,9},{9,8},{10,11... | collective-permute-start | bytes 884744 | tf_op jit(solution)/shard_map/ppermute | solution.py:28
  152.9 2.1 collective-permute-start.26
  170.1 51.5 %all-to-all-start.2 = ((bf16[16,72,768]{2,1,0:T(8,128)(2,1)}), bf16[16,72,768]{2,1,0:T(8,128)(2,1)S(1)}, u32[]{:S(2)}, u32[]{:S(2)}) async-start(bf16[16,72,768]{2,1,0:T(8,128)(2,1)} %bitcast.58), calls=%async_computation.2 | async-start | bytes 3538944 | tf_op jit(solution)/shard_map/all_to_all | solution.py:404
  178.0 9.2 %collective-permute-start.31 = (bf16[144,1024]{1,0:T(8,128)(2,1)S(1)}, bf16[144,1024]{1,0:T(8,128)(2,1)S(1)}, u32[]{:S(2)}, u32[]{:S(2)}) collective-permute-start(bf16[144,1024]{1,0:T(8,128)(2,1)S(1)} %shard_map.127.refs_26_.refs_0_), channel_id=1, source_target_pairs={{0,2},{1,3},{2,4},{3,5},{4,6},{5,7},{6,0},{7,1},{8,10},{9,11},{10,... | collective-permute-start | bytes 884744 | tf_op jit(solution)/shard_map/ppermute | solution.py:24
  178.1 15.5 %collective-permute-start.32 = (bf16[144,1024]{1,0:T(8,128)(2,1)S(1)}, bf16[144,1024]{1,0:T(8,128)(2,1)S(1)}, u32[]{:S(2)}, u32[]{:S(2)}) collective-permute-start(bf16[144,1024]{1,0:T(8,128)(2,1)S(1)} %shard_map.127.refs_26_.refs_0_), channel_id=1, source_target_pairs={{0,4},{1,5},{2,6},{3,7},{4,0},{5,1},{6,2},{7,3},{8,12},{9,13},{10,... | collective-permute-start | bytes 884744 | tf_op jit(solution)/shard_map/ppermute | solution.py:24
  181.0 14.3 %collective-permute-start.33 = (bf16[144,1024]{1,0:T(8,128)(2,1)S(1)}, bf16[144,1024]{1,0:T(8,128)(2,1)S(1)}, u32[]{:S(2)}, u32[]{:S(2)}) collective-permute-start(bf16[144,1024]{1,0:T(8,128)(2,1)S(1)} %shard_map.127.refs_26_.refs_0_), channel_id=1, source_target_pairs={{0,6},{1,7},{2,0},{3,1},{4,2},{5,3},{6,4},{7,5},{8,14},{9,15},{10,... | collective-permute-start | bytes 884744 | tf_op jit(solution)/shard_map/ppermute | solution.py:24
  181.0 24.1 %collective-permute-start.34 = (bf16[144,1024]{1,0:T(8,128)(2,1)S(1)}, bf16[144,1024]{1,0:T(8,128)(2,1)S(1)}, u32[]{:S(2)}, u32[]{:S(2)}) collective-permute-start(bf16[144,1024]{1,0:T(8,128)(2,1)S(1)} %shard_map.127.refs_26_.refs_0_), channel_id=1, source_target_pairs={{0,1},{1,0},{2,3},{3,2},{4,5},{5,4},{6,7},{7,6},{8,9},{9,8},{10,11... | collective-permute-start | bytes 884744 | tf_op jit(solution)/shard_map/ppermute | solution.py:28
  187.2 17.9 %collective-permute-start.35 = (bf16[144,1024]{1,0:T(8,128)(2,1)S(1)}, bf16[144,1024]{1,0:T(8,128)(2,1)S(1)}, u32[]{:S(2)}, u32[]{:S(2)}) collective-permute-start(bf16[144,1024]{1,0:T(8,128)(2,1)S(1)} %collective-permute-done.31.refs_1_), channel_id=1, source_target_pairs={{0,1},{1,0},{2,3},{3,2},{4,5},{5,4},{6,7},{7,6},{8,9},{9,8},{10,11... | collective-permute-start | bytes 884744 | tf_op jit(solution)/shard_map/ppermute | solution.py:28
  193.6 11.5 %collective-permute-start.36 = (bf16[144,1024]{1,0:T(8,128)(2,1)S(1)}, bf16[144,1024]{1,0:T(8,128)(2,1)S(1)}, u32[]{:S(2)}, u32[]{:S(2)}) collective-permute-start(bf16[144,1024]{1,0:T(8,128)(2,1)S(1)} %collective-permute-done.32.refs_2_), channel_id=1, source_target_pairs={{0,1},{1,0},{2,3},{3,2},{4,5},{5,4},{6,7},{7,6},{8,9},{9,8},{10,11... | collective-permute-start | bytes 884744 | tf_op jit(solution)/shard_map/ppermute | solution.py:28
  195.2 11.0 %collective-permute-start.37 = (bf16[144,1024]{1,0:T(8,128)(2,1)S(1)}, bf16[144,1024]{1,0:T(8,128)(2,1)S(1)}, u32[]{:S(2)}, u32[]{:S(2)}) collective-permute-start(bf16[144,1024]{1,0:T(8,128)(2,1)S(1)} %collective-permute-done.33.refs_3_), channel_id=1, source_target_pairs={{0,1},{1,0},{2,3},{3,2},{4,5},{5,4},{6,7},{7,6},{8,9},{9,8},{10,11... | collective-permute-start | bytes 884744 | tf_op jit(solution)/shard_map/ppermute | solution.py:28
  222.8 35.6 %all-to-all-start.3 = ((bf16[16,72,768]{2,1,0:T(8,128)(2,1)}), bf16[16,72,768]{2,1,0:T(8,128)(2,1)}, u32[]{:S(2)}, u32[]{:S(2)}) async-start(bf16[16,72,768]{2,1,0:T(8,128)(2,1)} %bitcast.59), calls=%async_computation.3 | async-start | bytes 3538944 | tf_op jit(solution)/shard_map/all_to_all | solution.py:404
  263.7 4.3 %collective-permute-start.38 = (bf16[4,128,768]{2,1,0:T(8,128)(2,1)S(1)}, bf16[4,128,768]{2,1,0:T(8,128)(2,1)S(1)}, u32[]{:S(2)}, u32[]{:S(2)}) collective-permute-start(bf16[4,128,768]{2,1,0:T(8,128)(2,1)S(1)} %bitcast.60), channel_id=1, source_target_pairs={{0,1},{1,0},{2,3},{3,2},{4,5},{5,4},{6,7},{7,6},{8,9},{9,8},{10,11... | collective-permute-start | bytes 2359304 | tf_op jit(solution)/shard_map/ppermute | solution.py:28
  265.2 6.8 %collective-permute-start.39 = (bf16[128,768]{1,0:T(8,128)(2,1)S(1)}, bf16[128,768]{1,0:T(8,128)(2,1)S(1)}, u32[]{:S(2)}, u32[]{:S(2)}) collective-permute-start(bf16[128,768]{1,0:T(8,128)(2,1)S(1)} %get-tuple-element.64), channel_id=1, source_target_pairs={{0,6},{1,7},{2,0},{3,1},{4,2},{5,3},{6,4},{7,5},{8,14},{9,15},{10,... | collective-permute-start | bytes 589832 | tf_op jit(solution)/shard_map/ppermute | solution.py:24
  267.4 12.4 %collective-permute-start.41 = (bf16[128,768]{1,0:T(8,128)(2,1)S(1)}, bf16[128,768]{1,0:T(8,128)(2,1)S(1)}, u32[]{:S(2)}, u32[]{:S(2)}) collective-permute-start(bf16[128,768]{1,0:T(8,128)(2,1)S(1)} %get-tuple-element.63), channel_id=1, source_target_pairs={{0,4},{1,5},{2,6},{3,7},{4,0},{5,1},{6,2},{7,3},{8,12},{9,13},{10,... | collective-permute-start | bytes 589832 | tf_op jit(solution)/shard_map/ppermute | solution.py:24
  267.4 15.6 %collective-permute-start.43 = (bf16[128,768]{1,0:T(8,128)(2,1)S(1)}, bf16[128,768]{1,0:T(8,128)(2,1)S(1)}, u32[]{:S(2)}, u32[]{:S(2)}) collective-permute-start(bf16[128,768]{1,0:T(8,128)(2,1)S(1)} %get-tuple-element.62), channel_id=1, source_target_pairs={{0,2},{1,3},{2,4},{3,5},{4,6},{5,7},{6,0},{7,1},{8,10},{9,11},{10,... | collective-permute-start | bytes 589832 | tf_op jit(solution)/shard_map/ppermute | solution.py:24
  268.1 11.7 %collective-permute-start.40 = (bf16[128,768]{1,0:T(8,128)(2,1)S(1)}, bf16[128,768]{1,0:T(8,128)(2,1)S(1)}, u32[]{:S(2)}, u32[]{:S(2)}) collective-permute-start(bf16[128,768]{1,0:T(8,128)(2,1)S(1)} %get-tuple-element.72), channel_id=1, source_target_pairs={{0,6},{1,7},{2,0},{3,1},{4,2},{5,3},{6,4},{7,5},{8,14},{9,15},{10,... | collective-permute-start | bytes 589832 | tf_op jit(solution)/shard_map/ppermute | solution.py:24
  270.2 12.8 %collective-permute-start.42 = (bf16[128,768]{1,0:T(8,128)(2,1)S(1)}, bf16[128,768]{1,0:T(8,128)(2,1)S(1)}, u32[]{:S(2)}, u32[]{:S(2)}) collective-permute-start(bf16[128,768]{1,0:T(8,128)(2,1)S(1)} %get-tuple-element.71), channel_id=1, source_target_pairs={{0,4},{1,5},{2,6},{3,7},{4,0},{5,1},{6,2},{7,3},{8,12},{9,13},{10,... | collective-permute-start | bytes 589832 | tf_op jit(solution)/shard_map/ppermute | solution.py:24
  272.0 15.7 %collective-permute-start.44 = (bf16[128,768]{1,0:T(8,128)(2,1)S(1)}, bf16[128,768]{1,0:T(8,128)(2,1)S(1)}, u32[]{:S(2)}, u32[]{:S(2)}) collective-permute-start(bf16[128,768]{1,0:T(8,128)(2,1)S(1)} %get-tuple-element.70), channel_id=1, source_target_pairs={{0,2},{1,3},{2,4},{3,5},{4,6},{5,7},{6,0},{7,1},{8,10},{9,11},{10,... | collective-permute-start | bytes 589832 | tf_op jit(solution)/shard_map/ppermute | solution.py:24
  (21 other events, 139.3 us)
where the time goes:
time: 294 us; the launch traced here: 289 us
  starting transfers between devices  92.6 us (31%)
  waiting for transfers between devices  91.1 us (31%)
  Pallas kernels  75.2 us (26%)
  matrix products  15.4 us (5%)
  local copies, waits for them, and re-layouts  9.5 us (3%)
  other arithmetic  3.74 us (1%)
    ppermute x25, waiting for transfers between devices, along_x(): return lax.ppermute(v, 'expert', pairs(dx, 0))  85.4 us
    pallas_call x12, Pallas kernels, call(): pl.pallas_call(kernel, grid_spec=pltpu.PrefetchScalarGridSpec(num_scalar_...  75.2 us
    ppermute x20, starting transfers between devices, swap_core(): return lax.ppermute(v, 'expert', pairs(0, 1))  32.8 us
    ppermute x25, starting transfers between devices, along_x(): return lax.ppermute(v, 'expert', pairs(dx, 0))  29.1 us
    all_to_all x2, starting transfers between devices, body(): lax.all_to_all(o.reshape(groups, splits * cap, cols), 'dp', split_axis=0,...  16 us
    dot_general x4, matrix products, dot(): lax.dot_general(a, b, (((ca,), (cb,)), ((), ())), preferred_element_type=...  15.4 us
    all_to_all x2, starting transfers between devices, give_back(): lax.all_to_all(slot_grad.reshape(groups, splits * cap, cols), 'dp', split...  14.7 us
    unnamed x48, local copies, waits for them, and re-layouts  8.23 us
  transfers between devices with their start and end apart: 49, of which 21 were waited for; matrix products, arithmetic and copies ran while one was open for 4% of the time, Pallas kernels for 18%

commit v1 on v0

--- a/solution.py
+++ b/solution.py
@@ -422,10 +422,15 @@
     returned1, grad_down, grad_gate, grad_up = lax.optimization_barrier(
         (returned1, grad_down, grad_gate, grad_up)
     )
-    back = [back0, dot(placed[1], returned1, 0, 0)]
-
-    combined = sum(back).astype(BF16).reshape(CORES, X_CHIPS, tokens, cols)
-    mine, other = combined[0], swap_core(combined[1])
+    half = X_CHIPS * tokens
+
+    def joined(low):
+        here = slice(low, low + half)
+        total = back0[here] + dot(placed[1][:, here], returned1, 0, 0)
+        return total.astype(BF16).reshape(X_CHIPS, tokens, cols)
+
+    other = swap_core(joined(half))
+    mine = joined(0)
     grad_input = jnp.zeros((tokens, width), BF16)
     for dx in range(X_CHIPS):
         for core, v in ((my_c, mine), (1 - my_c, other)):

time: 294 us -> 298 us (1.014)
  matrix products: 15.4 us -> 18.4 us
    dot_general x4 -> x5, matrix products: 15.4 us -> 18.4 us  [dot(): lax.dot_general(a, b, (((ca,), (cb,)), ((), ())), preferred_element_type=...]
    unnamed x48 -> x44, local copies, waits for them, and re-layouts: 8.23 us -> 6.56 us
  transfers between devices with their start and end apart: 49 -> 49, of which waited for: 21 -> 21; matrix products, arithmetic and copies ran while one was open for 4% -> 6% of each run, Pallas kernels for 18% -> 18%
where the time goes in v1:
time: 298 us; the launch traced here: 293 us
  starting transfers between devices  92.8 us (31%)
  waiting for transfers between devices  89.6 us (30%)
  Pallas kernels  75.1 us (25%)
  matrix products  18.4 us (6%)
  local copies, waits for them, and re-layouts  9.83 us (3%)
  other arithmetic  5.69 us (2%)
    ppermute x25, waiting for transfers between devices, along_x(): return lax.ppermute(v, 'expert', pairs(dx, 0))  84 us
    pallas_call x12, Pallas kernels, call(): pl.pallas_call(kernel, grid_spec=pltpu.PrefetchScalarGridSpec(num_scalar_...  75.1 us
    ppermute x20, starting transfers between devices, swap_core(): return lax.ppermute(v, 'expert', pairs(0, 1))  33.1 us
    ppermute x25, starting transfers between devices, along_x(): return lax.ppermute(v, 'expert', pairs(dx, 0))  29.1 us
    dot_general x5, matrix products, dot(): lax.dot_general(a, b, (((ca,), (cb,)), ((), ())), preferred_element_type=...  18.4 us
    all_to_all x2, starting transfers between devices, body(): lax.all_to_all(o.reshape(groups, splits * cap, cols), 'dp', split_axis=0,...  16 us
    all_to_all x2, starting transfers between devices, give_back(): lax.all_to_all(slot_grad.reshape(groups, splits * cap, cols), 'dp', split...  14.7 us
    unnamed x44, local copies, waits for them, and re-layouts  6.56 us
  transfers between devices with their start and end apart: 49, of which 21 were waited for; matrix products, arithmetic and copies ran while one was open for 6% of the time, Pallas kernels for 18%

profile of v1, /device:TPU:1, one launch (start us, length us, event | category | flops | bytes accessed | tf_op | source)
XLA Modules:
  0.0 293.0 jit_solution(14974276090396960766)
XLA Ops:
  3.7 1.9 multiply_convert_fusion
  5.9 2.1 collective-permute-start
  8.0 2.5 collective-permute-start.1
  13.3 4.9 %collective-permute-done = bf16[136,1536]{1,0:T(8,128)(2,1)S(1)} collective-permute-done((bf16[136,1536]{1,0:T(8,128)(2,1)S(1)}, bf16[136,1536]{1,0:T(8,128)(2,1)S(1)}, u32[]{:S(2)}, u32[]{:S(2)}) %collective-permute-start) | collective-permute-done | bytes 417824 | tf_op jit(solution)/shard_map/ppermute | solution.py:24
  18.2 1.8 collective-permute-start.4
  20.0 8.5 %collective-permute-done.1 = bf16[136,1536]{1,0:T(8,128)(2,1)S(1)} collective-permute-done((bf16[136,1536]{1,0:T(8,128)(2,1)S(1)}, bf16[136,1536]{1,0:T(8,128)(2,1)S(1)}, u32[]{:S(2)}, u32[]{:S(2)}) %collective-permute-start.1) | collective-permute-done | bytes 417824 | tf_op jit(solution)/shard_map/ppermute | solution.py:24
  36.5 3.7 %fusion.5 = bf16[1152,768]{1,0:T(8,128)(2,1)} fusion(bf16[1024,768]{1,0:T(8,128)(2,1)S(1)} %bitcast.53, s32[1024]{0:T(1024)S(1)} %bitcast.65, s32[1024]{0:T(1024)S(1)} %bitcast.61), kind=kOutput, calls=%fused_computation.6 | convolution fusion | flops 1816363008 | bytes 3350528 | tf_op jit(solution)/shard_map/dot_general | solution.py:32
  40.2 7.9 %all-to-all-start = ((bf16[16,72,768]{2,1,0:T(8,128)(2,1)}), bf16[16,72,768]{2,1,0:T(8,128)(2,1)}, u32[]{:S(2)}, u32[]{:S(2)}) async-start(bf16[16,72,768]{2,1,0:T(8,128)(2,1)} %bitcast.15), calls=%async_computation | async-start | bytes 3538944 | tf_op jit(solution)/shard_map/all_to_all | solution.py:372
  49.2 13.5 %collective-permute-done.10.b_ref.refs_14_.refs_15_ = bf16[2,2304,128]{2,1,0:T(8,128)(2,1)} collective-permute-done((bf16[2,2304,128]{2,1,0:T(8,128)(2,1)}, bf16[2,2304,128]{2,1,0:T(8,128)(2,1)}, u32[]{:S(2)}, u32[]{:S(2)}) %collective-permute-start.10) | collective-permute-done | bytes 1179680 | tf_op jit(solution)/shard_map/ppermute | solution.py:24
  66.4 2.7 shard_map.121
  69.0 2.7 collective-permute-start.13
  71.7 3.4 %convolution_convert_fusion = bf16[1152,768]{1,0:T(8,128)(2,1)} fusion(bf16[1024,768]{1,0:T(8,128)(2,1)S(1)} %bitcast.54, s32[1024]{0:T(1024)S(1)} %bitcast.66, s32[1024]{0:T(1024)S(1)} %bitcast.62, s32[1152]{0:T(1024)S(1)} %iota_add_fusion), kind=kOutput, calls=%fused_computation.7 | convolution fusion | flops 1816363008 | bytes 3355136 | tf_op jit(solution)/shard_map/dot_general | solution.py:32
  75.2 8.2 %all-to-all-start.1 = ((bf16[16,72,768]{2,1,0:T(8,128)(2,1)}), bf16[16,72,768]{2,1,0:T(8,128)(2,1)}, u32[]{:S(2)}, u32[]{:S(2)}) async-start(bf16[16,72,768]{2,1,0:T(8,128)(2,1)} %bitcast.58), calls=%async_computation.1 | async-start | bytes 3538944 | tf_op jit(solution)/shard_map/all_to_all | solution.py:372
  83.4 2.1 collective-permute-done.12.refs_3_.refs_12_
  85.5 6.7 %shard_map.122 = (f32[4,144,1024]{2,1,0:T(8,128)}, bf16[4,144,1024]{2,1,0:T(8,128)(2,1)S(1)}) custom-call(s32[2]{0:T(128)S(1)} %pad_add_fusion.where_ref, bf16[1152,768]{1,0:T(8,128)(2,1)} %bitcast.16.a_ref.d0_ref, bf16[2,1024,768]{2,1,0:T(8,128)(2,1)} %w_ref.3, bf16[2,2304,128]{2,1,0:T(8,128)(2,1)S(1)} %collective-permute-done.7.refs_0_.refs_16_.refs_17_, ...), custom_call_target="tpu_custom_call" | custom-call | flops 1000 | bytes 1000 | tf_op jit(solution)/shard_map/pallas_call | solution.py:36
  93.6 2.7 collective-permute-done.14.r_ref
  99.1 3.8 %collective-permute-start.16 = (bf16[144,1024]{1,0:T(8,128)(2,1)S(1)}, bf16[144,1024]{1,0:T(8,128)(2,1)S(1)}, u32[]{:S(2)}, u32[]{:S(2)}) collective-permute-start(bf16[144,1024]{1,0:T(8,128)(2,1)S(1)} %get-tuple-element.38), channel_id=1, source_target_pairs={{0,4},{1,5},{2,6},{3,7},{4,0},{5,1},{6,2},{7,3},{8,12},{9,13},{10,... | collective-permute-start | bytes 884744 | tf_op jit(solution)/shard_map/ppermute | solution.py:24
  103.0 5.7 %collective-permute-done.15.refs_0_ = bf16[144,1024]{1,0:T(8,128)(2,1)S(1)} collective-permute-done((bf16[144,1024]{1,0:T(8,128)(2,1)S(1)}, bf16[144,1024]{1,0:T(8,128)(2,1)S(1)}, u32[]{:S(2)}, u32[]{:S(2)}) %collective-permute-start.15) | collective-permute-done | bytes 294944 | tf_op jit(solution)/shard_map/ppermute | solution.py:24
  108.7 7.4 %collective-permute-done.16.refs_1_ = bf16[144,1024]{1,0:T(8,128)(2,1)S(1)} collective-permute-done((bf16[144,1024]{1,0:T(8,128)(2,1)S(1)}, bf16[144,1024]{1,0:T(8,128)(2,1)S(1)}, u32[]{:S(2)}, u32[]{:S(2)}) %collective-permute-start.16) | collective-permute-done | bytes 294944 | tf_op jit(solution)/shard_map/ppermute | solution.py:24
  116.8 5.6 %shard_map.125 = (f32[4,144,1024]{2,1,0:T(8,128)S(1)}, bf16[4,144,1024]{2,1,0:T(8,128)(2,1)S(1)}) custom-call(s32[2]{0:T(128)S(1)} %pad_add_fusion.where_ref, bf16[1152,768]{1,0:T(8,128)(2,1)} %bitcast.20.a_ref.d1_ref, bf16[2,1024,768]{2,1,0:T(8,128)(2,1)} %w_ref.3, bf16[144,1024]{1,0:T(8,128)(2,1)S(1)} %shard_map.124.refs_0_), custom_call_target="tpu_custom_call" | custom-call | flops 1000 | bytes 1000 | tf_op jit(solution)/shard_map/pallas_call | solution.py:36
  123.7 3.1 %collective-permute-start.21 = (bf16[144,1024]{1,0:T(8,128)(2,1)S(1)}, bf16[144,1024]{1,0:T(8,128)(2,1)S(1)}, u32[]{:S(2)}, u32[]{:S(2)}) collective-permute-start(bf16[144,1024]{1,0:T(8,128)(2,1)S(1)} %shard_map.124.refs_0_), channel_id=1, source_target_pairs={{0,4},{1,5},{2,6},{3,7},{4,0},{5,1},{6,2},{7,3},{8,12},{9,13},{10,... | collective-permute-start | bytes 884744 | tf_op jit(solution)/shard_map/ppermute | solution.py:24
  130.4 3.1 %collective-permute-done.20.refs_1_ = bf16[144,1024]{1,0:T(8,128)(2,1)S(1)} collective-permute-done((bf16[144,1024]{1,0:T(8,128)(2,1)S(1)}, bf16[144,1024]{1,0:T(8,128)(2,1)S(1)}, u32[]{:S(2)}, u32[]{:S(2)}) %collective-permute-start.20) | collective-permute-done | bytes 294944 | tf_op jit(solution)/shard_map/ppermute | solution.py:24
  133.5 1.8 collective-permute-start.23
  135.3 5.0 %collective-permute-done.21.refs_2_ = bf16[144,1024]{1,0:T(8,128)(2,1)S(1)} collective-permute-done((bf16[144,1024]{1,0:T(8,128)(2,1)S(1)}, bf16[144,1024]{1,0:T(8,128)(2,1)S(1)}, u32[]{:S(2)}, u32[]{:S(2)}) %collective-permute-start.21) | collective-permute-done | bytes 294944 | tf_op jit(solution)/shard_map/ppermute | solution.py:24
  140.3 1.8 collective-permute-start.24
  142.1 4.1 %collective-permute-done.28.refs_0_ = bf16[144,1024]{1,0:T(8,128)(2,1)S(1)} collective-permute-done((bf16[144,1024]{1,0:T(8,128)(2,1)S(1)}, bf16[144,1024]{1,0:T(8,128)(2,1)S(1)}, u32[]{:S(2)}, u32[]{:S(2)}) %collective-permute-start.28) | collective-permute-done | bytes 294944 | tf_op jit(solution)/shard_map/ppermute | solution.py:24
  147.1 5.9 %collective-permute-done.29.refs_1_ = bf16[144,1024]{1,0:T(8,128)(2,1)S(1)} collective-permute-done((bf16[144,1024]{1,0:T(8,128)(2,1)S(1)}, bf16[144,1024]{1,0:T(8,128)(2,1)S(1)}, u32[]{:S(2)}, u32[]{:S(2)}) %collective-permute-start.29) | collective-permute-done | bytes 294944 | tf_op jit(solution)/shard_map/ppermute | solution.py:24
  155.0 15.1 %shard_map.128 = (bf16[1152,1024]{1,0:T(8,128)(2,1)}, bf16[1152,1024]{1,0:T(8,128)(2,1)}, bf16[1152,1024]{1,0:T(8,128)(2,1)}, bf16[1152,768]{1,0:T(8,128)(2,1)}) custom-call(s32[2]{0:T(128)S(1)} %pad_add_fusion.where_ref, bf16[144,1024]{1,0:T(8,128)(2,1)S(1)} %shard_map.124.refs_0_, bf16[144,1024]{1,0:T(8,128)(2,1)S(1)} %collective-permute-done.20.refs_1_, ...), custom_call_target="tpu_custom_call" | custom-call | flops 1000 | bytes 50000000 | tf_op jit(solution)/shard_map/pallas_call | solution.py:36
  170.1 7.9 %all-to-all-start.2 = ((bf16[16,72,768]{2,1,0:T(8,128)(2,1)}), bf16[16,72,768]{2,1,0:T(8,128)(2,1)S(1)}, u32[]{:S(2)}, u32[]{:S(2)}) async-start(bf16[16,72,768]{2,1,0:T(8,128)(2,1)} %bitcast.59), calls=%async_computation.2 | async-start | bytes 3538944 | tf_op jit(solution)/shard_map/all_to_all | solution.py:404
  178.1 2.9 collective-permute-start.32
  182.3 4.9 %collective-permute-done.31.refs_1_ = bf16[144,1024]{1,0:T(8,128)(2,1)S(1)} collective-permute-done((bf16[144,1024]{1,0:T(8,128)(2,1)S(1)}, bf16[144,1024]{1,0:T(8,128)(2,1)S(1)}, u32[]{:S(2)}, u32[]{:S(2)}) %collective-permute-start.31) | collective-permute-done | bytes 294944 | tf_op jit(solution)/shard_map/ppermute | solution.py:24
  187.2 2.6 collective-permute-start.35
  189.7 3.8 %collective-permute-done.32.refs_2_ = bf16[144,1024]{1,0:T(8,128)(2,1)S(1)} collective-permute-done((bf16[144,1024]{1,0:T(8,128)(2,1)S(1)}, bf16[144,1024]{1,0:T(8,128)(2,1)S(1)}, u32[]{:S(2)}, u32[]{:S(2)}) %collective-permute-start.32) | collective-permute-done | bytes 294944 | tf_op jit(solution)/shard_map/ppermute | solution.py:24
  193.6 1.7 collective-permute-start.36
  195.2 10.1 %collective-permute-start.37 = (bf16[144,1024]{1,0:T(8,128)(2,1)S(1)}, bf16[144,1024]{1,0:T(8,128)(2,1)S(1)}, u32[]{:S(2)}, u32[]{:S(2)}) collective-permute-start(bf16[144,1024]{1,0:T(8,128)(2,1)S(1)} %collective-permute-done.33.refs_3_), channel_id=1, source_target_pairs={{0,1},{1,0},{2,3},{3,2},{4,5},{5,4},{6,7},{7,6},{8,9},{9,8},{10,11... | collective-permute-start | bytes 884744 | tf_op jit(solution)/shard_map/ppermute | solution.py:28
  206.6 15.2 %shard_map.129 = (bf16[1152,1024]{1,0:T(8,128)(2,1)}, bf16[1152,1024]{1,0:T(8,128)(2,1)}, bf16[1152,1024]{1,0:T(8,128)(2,1)}, bf16[1152,768]{1,0:T(8,128)(2,1)}) custom-call(s32[2]{0:T(128)S(1)} %pad_add_fusion.where_ref, bf16[144,1024]{1,0:T(8,128)(2,1)S(1)} %shard_map.127.refs_26_.refs_0_, bf16[144,1024]{1,0:T(8,128)(2,1)S(1)} %collective-permute-done.31.refs_1_, ...), custom_call_target="tpu_custom_call" | custom-call | flops 1000 | bytes 50000000 | tf_op jit(solution)/shard_map/pallas_call | solution.py:36
  223.1 6.8 %all-to-all-start.3 = ((bf16[16,72,768]{2,1,0:T(8,128)(2,1)}), bf16[16,72,768]{2,1,0:T(8,128)(2,1)}, u32[]{:S(2)}, u32[]{:S(2)}) async-start(bf16[16,72,768]{2,1,0:T(8,128)(2,1)} %bitcast.60), calls=%async_computation.3 | async-start | bytes 3538944 | tf_op jit(solution)/shard_map/all_to_all | solution.py:404
  229.8 1.9 compare_or_fusion
  231.8 10.7 %shard_map.130 = bf16[2,1024,768]{2,1,0:T(8,128)(2,1)} custom-call(s32[2]{0:T(128)S(1)} %pad_add_fusion.where_ref, bf16[1152,1024]{1,0:T(8,128)(2,1)S(1)} %copy-done.8, bf16[1152,1024]{1,0:T(8,128)(2,1)} %get-tuple-element.49.h1_ref, bf16[1152,768]{1,0:T(8,128)(2,1)} %bitcast.16.a_ref.d0_ref, bf16[1152,768]{1,0:T(8,128)(2,1)} %bitcast.20.a_ref.d1_ref), custom_call_target="tpu_custom_call" | custom-call | flops 1000 | bytes 1000 | tf_op jit(solution)/shard_map/pallas_call | solution.py:36
  242.5 4.1 %fusion.1.refs_0_ = f32[1024,768]{1,0:T(8,128)} fusion(bf16[1152,768]{1,0:T(8,128)(2,1)S(1)} %bitcast.57, s32[1024]{0:T(1024)S(1)} %bitcast.68, s32[1024]{0:T(1024)S(1)} %bitcast.64), kind=kOutput, calls=%fused_computation.4 | convolution fusion | flops 1815478272 | bytes 4923392 | tf_op jit(solution)/shard_map/dot_general | solution.py:32
  246.6 13.9 %shard_map.131 = (bf16[2,768,1024]{2,1,0:T(8,128)(2,1)}, bf16[2,768,1024]{2,1,0:T(8,128)(2,1)}) custom-call(s32[2]{0:T(128)S(1)} %pad_add_fusion.where_ref, bf16[2,1152,768]{2,1,0:T(8,128)(2,1)} %x_ref.1, bf16[1152,1024]{1,0:T(8,128)(2,1)S(1)} %copy-done.5, bf16[1152,1024]{1,0:T(8,128)(2,1)S(1)} %copy-done.6, bf16[1152,1024]{1,0:T(8,128)(2,1)} %get-tuple-element.52.dg1_ref, ...), custom_call_target="tpu_custom_call" | custom-call | flops 1000 | bytes 1000 | tf_op jit(solution)/shard_map/pallas_call | solution.py:36
  260.5 4.0 %fusion.16 = bf16[512,768]{1,0:T(8,128)(2,1)} fusion(f32[1024,768]{1,0:T(8,128)S(1)} %copy-done.11, bf16[1152,768]{1,0:T(8,128)(2,1)} %bitcast.24, pred[1152,1024]{1,0:T(32,128)(4,1)} %compare_or_fusion), kind=kOutput, calls=%fused_computation.18 | convolution fusion | flops 906756096 | bytes 4718592 | tf_op jit(solution)/shard_map/dot_general | solution.py:32
  265.2 3.1 %fusion.17 = bf16[512,768]{1,0:T(8,128)(2,1)S(1)} fusion(f32[1024,768]{1,0:T(8,128)S(1)} %copy-done.11, bf16[1152,768]{1,0:T(8,128)(2,1)} %bitcast.24, pred[1152,1024]{1,0:T(32,128)(4,1)} %compare_or_fusion), kind=kOutput, calls=%fused_computation.20 | convolution fusion | flops 906756096 | bytes 4718592 | tf_op jit(solution)/shard_map/dot_general | solution.py:32
  268.6 2.2 collective-permute-start.39
  272.7 2.1 collective-permute-start.40
  274.7 1.8 collective-permute-start.42
  279.1 8.6 %collective-permute-done.40 = bf16[128,768]{1,0:T(8,128)(2,1)S(1)} collective-permute-done((bf16[128,768]{1,0:T(8,128)(2,1)S(1)}, bf16[128,768]{1,0:T(8,128)(2,1)S(1)}, u32[]{:S(2)}, u32[]{:S(2)}) %collective-permute-start.40) | collective-permute-done | bytes 196640 | tf_op jit(solution)/shard_map/ppermute | solution.py:24
  287.8 3.9 %collective-permute-done.44 = bf16[128,768]{1,0:T(8,128)(2,1)S(1)} collective-permute-done((bf16[128,768]{1,0:T(8,128)(2,1)S(1)}, bf16[128,768]{1,0:T(8,128)(2,1)S(1)}, u32[]{:S(2)}, u32[]{:S(2)}) %collective-permute-start.44) | collective-permute-done | bytes 196640 | tf_op jit(solution)/shard_map/ppermute | solution.py:24
  (149 shorter events, 41.9 us)
Async XLA Ops:
  5.9 12.3 %collective-permute-start = (bf16[136,1536]{1,0:T(8,128)(2,1)S(1)}, bf16[136,1536]{1,0:T(8,128)(2,1)S(1)}, u32[]{:S(2)}, u32[]{:S(2)}) collective-permute-start(bf16[136,1536]{1,0:T(8,128)(2,1)S(1)} %get-tuple-element.74), channel_id=1, source_target_pairs={{0,2},{1,3},{2,4},{3,5},{4,6},{5,7},{6,0},{7,1},{8,10},{9,11},{10,... | collective-permute-start | bytes 1253384 | tf_op jit(solution)/shard_map/ppermute | solution.py:24
  8.0 20.4 %collective-permute-start.1 = (bf16[136,1536]{1,0:T(8,128)(2,1)S(1)}, bf16[136,1536]{1,0:T(8,128)(2,1)S(1)}, u32[]{:S(2)}, u32[]{:S(2)}) collective-permute-start(bf16[136,1536]{1,0:T(8,128)(2,1)S(1)} %get-tuple-element.75), channel_id=1, source_target_pairs={{0,4},{1,5},{2,6},{3,7},{4,0},{5,1},{6,2},{7,3},{8,12},{9,13},{10,... | collective-permute-start | bytes 1253384 | tf_op jit(solution)/shard_map/ppermute | solution.py:24
  10.4 19.6 %collective-permute-start.2 = (bf16[136,1536]{1,0:T(8,128)(2,1)S(1)}, bf16[136,1536]{1,0:T(8,128)(2,1)S(1)}, u32[]{:S(2)}, u32[]{:S(2)}) collective-permute-start(bf16[136,1536]{1,0:T(8,128)(2,1)S(1)} %get-tuple-element.73), channel_id=1, source_target_pairs={{0,6},{1,7},{2,0},{3,1},{4,2},{5,3},{6,4},{7,5},{8,14},{9,15},{10,... | collective-permute-start | bytes 1253384 | tf_op jit(solution)/shard_map/ppermute | solution.py:24
  11.6 18.7 %collective-permute-start.3 = (bf16[136,768]{1,0:T(8,128)(2,1)S(1)}, bf16[136,768]{1,0:T(8,128)(2,1)S(1)}, u32[]{:S(2)}, u32[]{:S(2)}) collective-permute-start(bf16[136,768]{1,0:T(8,128)(2,1)S(1)} %constant_dynamic-slice_fusion.3), channel_id=1, source_target_pairs={{0,1},{1,0},{2,3},{3,2},{4,5},{5,4},{6,7},{7,6},{8,9},{9,8},{10,11... | collective-permute-start | bytes 626696 | tf_op jit(solution)/shard_map/ppermute | solution.py:28
  18.2 12.1 %collective-permute-start.4 = (bf16[136,768]{1,0:T(8,128)(2,1)S(1)}, bf16[136,768]{1,0:T(8,128)(2,1)S(1)}, u32[]{:S(2)}, u32[]{:S(2)}) collective-permute-start(bf16[136,768]{1,0:T(8,128)(2,1)S(1)} %constant_dynamic-slice_fusion.2), channel_id=1, source_target_pairs={{0,1},{1,0},{2,3},{3,2},{4,5},{5,4},{6,7},{7,6},{8,9},{9,8},{10,11... | collective-permute-start | bytes 626696 | tf_op jit(solution)/shard_map/ppermute | solution.py:28
  28.5 2.7 collective-permute-start.5
  35.0 27.7 %collective-permute-start.10 = (bf16[2,2304,128]{2,1,0:T(8,128)(2,1)}, bf16[2,2304,128]{2,1,0:T(8,128)(2,1)}, u32[]{:S(2)}, u32[]{:S(2)}) collective-permute-start(bf16[2,2304,128]{2,1,0:T(8,128)(2,1)} %shard_map.120.refs_8_.refs_9_), channel_id=1, source_target_pairs={{0,6},{1,7},{2,0},{3,1},{4,2},{5,3},{6,4},{7,5},{8,14},{9,15},{10,... | collective-permute-start | bytes 3538952 | tf_op jit(solution)/shard_map/ppermute | solution.py:24
  36.4 28.4 %collective-permute-start.8 = (bf16[2,2304,128]{2,1,0:T(8,128)(2,1)}, bf16[2,2304,128]{2,1,0:T(8,128)(2,1)}, u32[]{:S(2)}, u32[]{:S(2)}) collective-permute-start(bf16[2,2304,128]{2,1,0:T(8,128)(2,1)} %shard_map.120.refs_8_.refs_9_), channel_id=1, source_target_pairs={{0,2},{1,3},{2,4},{3,5},{4,6},{5,7},{6,0},{7,1},{8,10},{9,11},{10,... | collective-permute-start | bytes 3538952 | tf_op jit(solution)/shard_map/ppermute | solution.py:24
  40.2 34.9 %all-to-all-start = ((bf16[16,72,768]{2,1,0:T(8,128)(2,1)}), bf16[16,72,768]{2,1,0:T(8,128)(2,1)}, u32[]{:S(2)}, u32[]{:S(2)}) async-start(bf16[16,72,768]{2,1,0:T(8,128)(2,1)} %bitcast.15), calls=%async_computation | async-start | bytes 3538944 | tf_op jit(solution)/shard_map/all_to_all | solution.py:372
  48.1 35.2 %collective-permute-start.7 = (bf16[2,2304,128]{2,1,0:T(8,128)(2,1)}, bf16[2,2304,128]{2,1,0:T(8,128)(2,1)S(1)}, u32[]{:S(2)}, u32[]{:S(2)}) collective-permute-start(bf16[2,2304,128]{2,1,0:T(8,128)(2,1)} %shard_map.120.refs_8_.refs_9_), channel_id=1, source_target_pairs={{0,1},{1,0},{2,3},{3,2},{4,5},{5,4},{6,7},{7,6},{8,9},{9,8},{10,11... | collective-permute-start | bytes 3538952 | tf_op jit(solution)/shard_map/ppermute | solution.py:28
  62.7 22.8 %collective-permute-start.11 = (bf16[2,2304,128]{2,1,0:T(8,128)(2,1)}, bf16[2,2304,128]{2,1,0:T(8,128)(2,1)S(1)}, u32[]{:S(2)}, u32[]{:S(2)}) collective-permute-start(bf16[2,2304,128]{2,1,0:T(8,128)(2,1)} %collective-permute-done.10.b_ref.refs_14_.refs_15_), channel_id=1, source_target_pairs={{0,1},{1,0},{2,3},{3,2},{4,5},{5,4},{6,7},{7,6},{8,9},{9,8},{10,11... | collective-permute-start | bytes 3538952 | tf_op jit(solution)/shard_map/ppermute | solution.py:28
  64.8 20.7 %collective-permute-start.9 = (bf16[2,2304,128]{2,1,0:T(8,128)(2,1)}, bf16[2,2304,128]{2,1,0:T(8,128)(2,1)S(1)}, u32[]{:S(2)}, u32[]{:S(2)}) collective-permute-start(bf16[2,2304,128]{2,1,0:T(8,128)(2,1)} %collective-permute-done.8.a_ref.refs_10_.refs_11_), channel_id=1, source_target_pairs={{0,1},{1,0},{2,3},{3,2},{4,5},{5,4},{6,7},{7,6},{8,9},{9,8},{10,11... | collective-permute-start | bytes 3538952 | tf_op jit(solution)/shard_map/ppermute | solution.py:28
  69.0 16.5 %collective-permute-start.12 = (bf16[2304,128]{1,0:T(8,128)(2,1)}, bf16[2304,128]{1,0:T(8,128)(2,1)}, u32[]{:S(2)}, u32[]{:S(2)}) collective-permute-start(bf16[2304,128]{1,0:T(8,128)(2,1)} %get-tuple-element.32), channel_id=1, source_target_pairs={{0,2},{1,3},{2,4},{3,5},{4,6},{5,7},{6,0},{7,1},{8,10},{9,11},{10,... | collective-permute-start | bytes 1769480 | tf_op jit(solution)/shard_map/ppermute | solution.py:24
  69.0 16.5 %collective-permute-start.13 = (bf16[2304,128]{1,0:T(8,128)(2,1)}, bf16[2304,128]{1,0:T(8,128)(2,1)}, u32[]{:S(2)}, u32[]{:S(2)}) collective-permute-start(bf16[2304,128]{1,0:T(8,128)(2,1)} %get-tuple-element.33), channel_id=1, source_target_pairs={{0,6},{1,7},{2,0},{3,1},{4,2},{5,3},{6,4},{7,5},{8,14},{9,15},{10,... | collective-permute-start | bytes 1769480 | tf_op jit(solution)/shard_map/ppermute | solution.py:24
  75.2 41.6 %all-to-all-start.1 = ((bf16[16,72,768]{2,1,0:T(8,128)(2,1)}), bf16[16,72,768]{2,1,0:T(8,128)(2,1)}, u32[]{:S(2)}, u32[]{:S(2)}) async-start(bf16[16,72,768]{2,1,0:T(8,128)(2,1)} %bitcast.58), calls=%async_computation.1 | async-start | bytes 3538944 | tf_op jit(solution)/shard_map/all_to_all | solution.py:372
  92.2 4.1 %collective-permute-start.14 = (bf16[4,144,1024]{2,1,0:T(8,128)(2,1)S(1)}, bf16[4,144,1024]{2,1,0:T(8,128)(2,1)S(1)}, u32[]{:S(2)}, u32[]{:S(2)}) collective-permute-start(bf16[4,144,1024]{2,1,0:T(8,128)(2,1)S(1)} %get-tuple-element.35), channel_id=1, source_target_pairs={{0,1},{1,0},{2,3},{3,2},{4,5},{5,4},{6,7},{7,6},{8,9},{9,8},{10,11... | collective-permute-start | bytes 3538952 | tf_op jit(solution)/shard_map/ppermute | solution.py:28
  93.1 9.9 %collective-permute-start.18 = (bf16[2304,128]{1,0:T(8,128)(2,1)}, bf16[2304,128]{1,0:T(8,128)(2,1)S(1)}, u32[]{:S(2)}, u32[]{:S(2)}) collective-permute-start(bf16[2304,128]{1,0:T(8,128)(2,1)} %collective-permute-done.12.refs_3_.refs_12_), channel_id=1, source_target_pairs={{0,1},{1,0},{2,3},{3,2},{4,5},{5,4},{6,7},{7,6},{8,9},{9,8},{10,11... | collective-permute-start | bytes 1769480 | tf_op jit(solution)/shard_map/ppermute | solution.py:28
  93.2 9.8 %collective-permute-start.19 = (bf16[2304,128]{1,0:T(8,128)(2,1)}, bf16[2304,128]{1,0:T(8,128)(2,1)S(1)}, u32[]{:S(2)}, u32[]{:S(2)}) collective-permute-start(bf16[2304,128]{1,0:T(8,128)(2,1)} %collective-permute-done.13.refs_4_.refs_13_), channel_id=1, source_target_pairs={{0,1},{1,0},{2,3},{3,2},{4,5},{5,4},{6,7},{7,6},{8,9},{9,8},{10,11... | collective-permute-start | bytes 1769480 | tf_op jit(solution)/shard_map/ppermute | solution.py:28
  99.1 9.6 %collective-permute-start.15 = (bf16[144,1024]{1,0:T(8,128)(2,1)S(1)}, bf16[144,1024]{1,0:T(8,128)(2,1)S(1)}, u32[]{:S(2)}, u32[]{:S(2)}) collective-permute-start(bf16[144,1024]{1,0:T(8,128)(2,1)S(1)} %get-tuple-element.37), channel_id=1, source_target_pairs={{0,2},{1,3},{2,4},{3,5},{4,6},{5,7},{6,0},{7,1},{8,10},{9,11},{10,... | collective-permute-start | bytes 884744 | tf_op jit(solution)/shard_map/ppermute | solution.py:24
  99.1 16.9 %collective-permute-start.16 = (bf16[144,1024]{1,0:T(8,128)(2,1)S(1)}, bf16[144,1024]{1,0:T(8,128)(2,1)S(1)}, u32[]{:S(2)}, u32[]{:S(2)}) collective-permute-start(bf16[144,1024]{1,0:T(8,128)(2,1)S(1)} %get-tuple-element.38), channel_id=1, source_target_pairs={{0,4},{1,5},{2,6},{3,7},{4,0},{5,1},{6,2},{7,3},{8,12},{9,13},{10,... | collective-permute-start | bytes 884744 | tf_op jit(solution)/shard_map/ppermute | solution.py:24
  103.0 13.1 %collective-permute-start.17 = (bf16[144,1024]{1,0:T(8,128)(2,1)S(1)}, bf16[144,1024]{1,0:T(8,128)(2,1)S(1)}, u32[]{:S(2)}, u32[]{:S(2)}) collective-permute-start(bf16[144,1024]{1,0:T(8,128)(2,1)S(1)} %get-tuple-element.39), channel_id=1, source_target_pairs={{0,6},{1,7},{2,0},{3,1},{4,2},{5,3},{6,4},{7,5},{8,14},{9,15},{10,... | collective-permute-start | bytes 884744 | tf_op jit(solution)/shard_map/ppermute | solution.py:24
  122.5 4.4 %collective-permute-start.27 = (bf16[4,144,1024]{2,1,0:T(8,128)(2,1)S(1)}, bf16[4,144,1024]{2,1,0:T(8,128)(2,1)S(1)}, u32[]{:S(2)}, u32[]{:S(2)}) collective-permute-start(bf16[4,144,1024]{2,1,0:T(8,128)(2,1)S(1)} %get-tuple-element.41), channel_id=1, source_target_pairs={{0,1},{1,0},{2,3},{3,2},{4,5},{5,4},{6,7},{7,6},{8,9},{9,8},{10,11... | collective-permute-start | bytes 3538952 | tf_op jit(solution)/shard_map/ppermute | solution.py:28
  123.7 9.8 %collective-permute-start.20 = (bf16[144,1024]{1,0:T(8,128)(2,1)S(1)}, bf16[144,1024]{1,0:T(8,128)(2,1)S(1)}, u32[]{:S(2)}, u32[]{:S(2)}) collective-permute-start(bf16[144,1024]{1,0:T(8,128)(2,1)S(1)} %shard_map.124.refs_0_), channel_id=1, source_target_pairs={{0,2},{1,3},{2,4},{3,5},{4,6},{5,7},{6,0},{7,1},{8,10},{9,11},{10,... | collective-permute-start | bytes 884744 | tf_op jit(solution)/shard_map/ppermute | solution.py:24
  123.7 16.5 %collective-permute-start.21 = (bf16[144,1024]{1,0:T(8,128)(2,1)S(1)}, bf16[144,1024]{1,0:T(8,128)(2,1)S(1)}, u32[]{:S(2)}, u32[]{:S(2)}) collective-permute-start(bf16[144,1024]{1,0:T(8,128)(2,1)S(1)} %shard_map.124.refs_0_), channel_id=1, source_target_pairs={{0,4},{1,5},{2,6},{3,7},{4,0},{5,1},{6,2},{7,3},{8,12},{9,13},{10,... | collective-permute-start | bytes 884744 | tf_op jit(solution)/shard_map/ppermute | solution.py:24
  126.8 13.5 %collective-permute-start.22 = (bf16[144,1024]{1,0:T(8,128)(2,1)S(1)}, bf16[144,1024]{1,0:T(8,128)(2,1)S(1)}, u32[]{:S(2)}, u32[]{:S(2)}) collective-permute-start(bf16[144,1024]{1,0:T(8,128)(2,1)S(1)} %shard_map.124.refs_0_), channel_id=1, source_target_pairs={{0,6},{1,7},{2,0},{3,1},{4,2},{5,3},{6,4},{7,5},{8,14},{9,15},{10,... | collective-permute-start | bytes 884744 | tf_op jit(solution)/shard_map/ppermute | solution.py:24
  127.9 18.3 %collective-permute-start.28 = (bf16[144,1024]{1,0:T(8,128)(2,1)S(1)}, bf16[144,1024]{1,0:T(8,128)(2,1)S(1)}, u32[]{:S(2)}, u32[]{:S(2)}) collective-permute-start(bf16[144,1024]{1,0:T(8,128)(2,1)S(1)} %get-tuple-element.43), channel_id=1, source_target_pairs={{0,2},{1,3},{2,4},{3,5},{4,6},{5,7},{6,0},{7,1},{8,10},{9,11},{10,... | collective-permute-start | bytes 884744 | tf_op jit(solution)/shard_map/ppermute | solution.py:24
  129.4 23.5 %collective-permute-start.29 = (bf16[144,1024]{1,0:T(8,128)(2,1)S(1)}, bf16[144,1024]{1,0:T(8,128)(2,1)S(1)}, u32[]{:S(2)}, u32[]{:S(2)}) collective-permute-start(bf16[144,1024]{1,0:T(8,128)(2,1)S(1)} %get-tuple-element.44), channel_id=1, source_target_pairs={{0,4},{1,5},{2,6},{3,7},{4,0},{5,1},{6,2},{7,3},{8,12},{9,13},{10,... | collective-permute-start | bytes 884744 | tf_op jit(solution)/shard_map/ppermute | solution.py:24
  133.5 21.0 %collective-permute-start.23 = (bf16[144,1024]{1,0:T(8,128)(2,1)S(1)}, bf16[144,1024]{1,0:T(8,128)(2,1)S(1)}, u32[]{:S(2)}, u32[]{:S(2)}) collective-permute-start(bf16[144,1024]{1,0:T(8,128)(2,1)S(1)} %shard_map.124.refs_0_), channel_id=1, source_target_pairs={{0,1},{1,0},{2,3},{3,2},{4,5},{5,4},{6,7},{7,6},{8,9},{9,8},{10,11... | collective-permute-start | bytes 884744 | tf_op jit(solution)/shard_map/ppermute | solution.py:28
  140.3 13.5 %collective-permute-start.30 = (bf16[144,1024]{1,0:T(8,128)(2,1)S(1)}, bf16[144,1024]{1,0:T(8,128)(2,1)S(1)}, u32[]{:S(2)}, u32[]{:S(2)}) collective-permute-start(bf16[144,1024]{1,0:T(8,128)(2,1)S(1)} %get-tuple-element.45), channel_id=1, source_target_pairs={{0,6},{1,7},{2,0},{3,1},{4,2},{5,3},{6,4},{7,5},{8,14},{9,15},{10,... | collective-permute-start | bytes 884744 | tf_op jit(solution)/shard_map/ppermute | solution.py:24
  140.3 14.2 %collective-permute-start.24 = (bf16[144,1024]{1,0:T(8,128)(2,1)S(1)}, bf16[144,1024]{1,0:T(8,128)(2,1)S(1)}, u32[]{:S(2)}, u32[]{:S(2)}) collective-permute-start(bf16[144,1024]{1,0:T(8,128)(2,1)S(1)} %collective-permute-done.20.refs_1_), channel_id=1, source_target_pairs={{0,1},{1,0},{2,3},{3,2},{4,5},{5,4},{6,7},{7,6},{8,9},{9,8},{10,11... | collective-permute-start | bytes 884744 | tf_op jit(solution)/shard_map/ppermute | solution.py:28
  146.2 8.4 %collective-permute-start.25 = (bf16[144,1024]{1,0:T(8,128)(2,1)S(1)}, bf16[144,1024]{1,0:T(8,128)(2,1)S(1)}, u32[]{:S(2)}, u32[]{:S(2)}) collective-permute-start(bf16[144,1024]{1,0:T(8,128)(2,1)S(1)} %collective-permute-done.21.refs_2_), channel_id=1, source_target_pairs={{0,1},{1,0},{2,3},{3,2},{4,5},{5,4},{6,7},{7,6},{8,9},{9,8},{10,11... | collective-permute-start | bytes 884744 | tf_op jit(solution)/shard_map/ppermute | solution.py:28
  152.9 2.1 collective-permute-start.26
  170.1 51.7 %all-to-all-start.2 = ((bf16[16,72,768]{2,1,0:T(8,128)(2,1)}), bf16[16,72,768]{2,1,0:T(8,128)(2,1)S(1)}, u32[]{:S(2)}, u32[]{:S(2)}) async-start(bf16[16,72,768]{2,1,0:T(8,128)(2,1)} %bitcast.59), calls=%async_computation.2 | async-start | bytes 3538944 | tf_op jit(solution)/shard_map/all_to_all | solution.py:404
  178.0 9.2 %collective-permute-start.31 = (bf16[144,1024]{1,0:T(8,128)(2,1)S(1)}, bf16[144,1024]{1,0:T(8,128)(2,1)S(1)}, u32[]{:S(2)}, u32[]{:S(2)}) collective-permute-start(bf16[144,1024]{1,0:T(8,128)(2,1)S(1)} %shard_map.127.refs_26_.refs_0_), channel_id=1, source_target_pairs={{0,2},{1,3},{2,4},{3,5},{4,6},{5,7},{6,0},{7,1},{8,10},{9,11},{10,... | collective-permute-start | bytes 884744 | tf_op jit(solution)/shard_map/ppermute | solution.py:24
  178.1 15.5 %collective-permute-start.32 = (bf16[144,1024]{1,0:T(8,128)(2,1)S(1)}, bf16[144,1024]{1,0:T(8,128)(2,1)S(1)}, u32[]{:S(2)}, u32[]{:S(2)}) collective-permute-start(bf16[144,1024]{1,0:T(8,128)(2,1)S(1)} %shard_map.127.refs_26_.refs_0_), channel_id=1, source_target_pairs={{0,4},{1,5},{2,6},{3,7},{4,0},{5,1},{6,2},{7,3},{8,12},{9,13},{10,... | collective-permute-start | bytes 884744 | tf_op jit(solution)/shard_map/ppermute | solution.py:24
  181.0 14.3 %collective-permute-start.33 = (bf16[144,1024]{1,0:T(8,128)(2,1)S(1)}, bf16[144,1024]{1,0:T(8,128)(2,1)S(1)}, u32[]{:S(2)}, u32[]{:S(2)}) collective-permute-start(bf16[144,1024]{1,0:T(8,128)(2,1)S(1)} %shard_map.127.refs_26_.refs_0_), channel_id=1, source_target_pairs={{0,6},{1,7},{2,0},{3,1},{4,2},{5,3},{6,4},{7,5},{8,14},{9,15},{10,... | collective-permute-start | bytes 884744 | tf_op jit(solution)/shard_map/ppermute | solution.py:24
  181.0 24.4 %collective-permute-start.34 = (bf16[144,1024]{1,0:T(8,128)(2,1)S(1)}, bf16[144,1024]{1,0:T(8,128)(2,1)S(1)}, u32[]{:S(2)}, u32[]{:S(2)}) collective-permute-start(bf16[144,1024]{1,0:T(8,128)(2,1)S(1)} %shard_map.127.refs_26_.refs_0_), channel_id=1, source_target_pairs={{0,1},{1,0},{2,3},{3,2},{4,5},{5,4},{6,7},{7,6},{8,9},{9,8},{10,11... | collective-permute-start | bytes 884744 | tf_op jit(solution)/shard_map/ppermute | solution.py:28
  187.2 18.2 %collective-permute-start.35 = (bf16[144,1024]{1,0:T(8,128)(2,1)S(1)}, bf16[144,1024]{1,0:T(8,128)(2,1)S(1)}, u32[]{:S(2)}, u32[]{:S(2)}) collective-permute-start(bf16[144,1024]{1,0:T(8,128)(2,1)S(1)} %collective-permute-done.31.refs_1_), channel_id=1, source_target_pairs={{0,1},{1,0},{2,3},{3,2},{4,5},{5,4},{6,7},{7,6},{8,9},{9,8},{10,11... | collective-permute-start | bytes 884744 | tf_op jit(solution)/shard_map/ppermute | solution.py:28
  193.6 11.8 %collective-permute-start.36 = (bf16[144,1024]{1,0:T(8,128)(2,1)S(1)}, bf16[144,1024]{1,0:T(8,128)(2,1)S(1)}, u32[]{:S(2)}, u32[]{:S(2)}) collective-permute-start(bf16[144,1024]{1,0:T(8,128)(2,1)S(1)} %collective-permute-done.32.refs_2_), channel_id=1, source_target_pairs={{0,1},{1,0},{2,3},{3,2},{4,5},{5,4},{6,7},{7,6},{8,9},{9,8},{10,11... | collective-permute-start | bytes 884744 | tf_op jit(solution)/shard_map/ppermute | solution.py:28
  195.2 11.3 %collective-permute-start.37 = (bf16[144,1024]{1,0:T(8,128)(2,1)S(1)}, bf16[144,1024]{1,0:T(8,128)(2,1)S(1)}, u32[]{:S(2)}, u32[]{:S(2)}) collective-permute-start(bf16[144,1024]{1,0:T(8,128)(2,1)S(1)} %collective-permute-done.33.refs_3_), channel_id=1, source_target_pairs={{0,1},{1,0},{2,3},{3,2},{4,5},{5,4},{6,7},{7,6},{8,9},{9,8},{10,11... | collective-permute-start | bytes 884744 | tf_op jit(solution)/shard_map/ppermute | solution.py:28
  223.1 37.5 %all-to-all-start.3 = ((bf16[16,72,768]{2,1,0:T(8,128)(2,1)}), bf16[16,72,768]{2,1,0:T(8,128)(2,1)}, u32[]{:S(2)}, u32[]{:S(2)}) async-start(bf16[16,72,768]{2,1,0:T(8,128)(2,1)} %bitcast.60), calls=%async_computation.3 | async-start | bytes 3538944 | tf_op jit(solution)/shard_map/all_to_all | solution.py:404
  264.6 6.9 %collective-permute-start.38 = (bf16[4,128,768]{2,1,0:T(8,128)(2,1)}, bf16[4,128,768]{2,1,0:T(8,128)(2,1)}, u32[]{:S(2)}, u32[]{:S(2)}) collective-permute-start(bf16[4,128,768]{2,1,0:T(8,128)(2,1)} %bitcast.25), channel_id=1, source_target_pairs={{0,1},{1,0},{2,3},{3,2},{4,5},{5,4},{6,7},{7,6},{8,9},{9,8},{10,11... | collective-permute-start | bytes 2359304 | tf_op jit(solution)/shard_map/ppermute | solution.py:28
  268.6 10.4 %collective-permute-start.39 = (bf16[128,768]{1,0:T(8,128)(2,1)S(1)}, bf16[128,768]{1,0:T(8,128)(2,1)S(1)}, u32[]{:S(2)}, u32[]{:S(2)}) collective-permute-start(bf16[128,768]{1,0:T(8,128)(2,1)S(1)} %get-tuple-element.71), channel_id=1, source_target_pairs={{0,6},{1,7},{2,0},{3,1},{4,2},{5,3},{6,4},{7,5},{8,14},{9,15},{10,... | collective-permute-start | bytes 589832 | tf_op jit(solution)/shard_map/ppermute | solution.py:24
  270.8 16.9 %collective-permute-start.41 = (bf16[128,768]{1,0:T(8,128)(2,1)S(1)}, bf16[128,768]{1,0:T(8,128)(2,1)S(1)}, u32[]{:S(2)}, u32[]{:S(2)}) collective-permute-start(bf16[128,768]{1,0:T(8,128)(2,1)S(1)} %get-tuple-element.70), channel_id=1, source_target_pairs={{0,4},{1,5},{2,6},{3,7},{4,0},{5,1},{6,2},{7,3},{8,12},{9,13},{10,... | collective-permute-start | bytes 589832 | tf_op jit(solution)/shard_map/ppermute | solution.py:24
  270.8 16.9 %collective-permute-start.43 = (bf16[128,768]{1,0:T(8,128)(2,1)S(1)}, bf16[128,768]{1,0:T(8,128)(2,1)S(1)}, u32[]{:S(2)}, u32[]{:S(2)}) collective-permute-start(bf16[128,768]{1,0:T(8,128)(2,1)S(1)} %get-tuple-element.69), channel_id=1, source_target_pairs={{0,2},{1,3},{2,4},{3,5},{4,6},{5,7},{6,0},{7,1},{8,10},{9,11},{10,... | collective-permute-start | bytes 589832 | tf_op jit(solution)/shard_map/ppermute | solution.py:24
  272.7 15.0 %collective-permute-start.40 = (bf16[128,768]{1,0:T(8,128)(2,1)S(1)}, bf16[128,768]{1,0:T(8,128)(2,1)S(1)}, u32[]{:S(2)}, u32[]{:S(2)}) collective-permute-start(bf16[128,768]{1,0:T(8,128)(2,1)S(1)} %get-tuple-element.68), channel_id=1, source_target_pairs={{0,6},{1,7},{2,0},{3,1},{4,2},{5,3},{6,4},{7,5},{8,14},{9,15},{10,... | collective-permute-start | bytes 589832 | tf_op jit(solution)/shard_map/ppermute | solution.py:24
  274.7 13.0 %collective-permute-start.42 = (bf16[128,768]{1,0:T(8,128)(2,1)S(1)}, bf16[128,768]{1,0:T(8,128)(2,1)S(1)}, u32[]{:S(2)}, u32[]{:S(2)}) collective-permute-start(bf16[128,768]{1,0:T(8,128)(2,1)S(1)} %get-tuple-element.67), channel_id=1, source_target_pairs={{0,4},{1,5},{2,6},{3,7},{4,0},{5,1},{6,2},{7,3},{8,12},{9,13},{10,... | collective-permute-start | bytes 589832 | tf_op jit(solution)/shard_map/ppermute | solution.py:24
  279.0 12.6 %collective-permute-start.44 = (bf16[128,768]{1,0:T(8,128)(2,1)S(1)}, bf16[128,768]{1,0:T(8,128)(2,1)S(1)}, u32[]{:S(2)}, u32[]{:S(2)}) collective-permute-start(bf16[128,768]{1,0:T(8,128)(2,1)S(1)} %get-tuple-element.66), channel_id=1, source_target_pairs={{0,2},{1,3},{2,4},{3,5},{4,6},{5,7},{6,0},{7,1},{8,10},{9,11},{10,... | collective-permute-start | bytes 589832 | tf_op jit(solution)/shard_map/ppermute | solution.py:24
  (19 other events, 134.7 us)
